TPU v7x, 256 devices: a whole 4x4x8 slice. The times are simulated.
256 devices in a mesh: pair: 32 (over z, y), row: 8 (over x, core).
Axes of the slice: x: 4, y: 4, z: 8, core: 2. Of those that a mesh axis runs over, the one named last changes fastest.
Arguments:
- matrix: float32 [32768, 8192], P('row', 'pair'), may hold values from -54 to 54
Outputs:
- magnitudes: float32 [32768, 8192], P('row', 'pair')
- energies: float32 [8192], P('pair')
All inputs are finite; a program needn't handle non-finite values.
Results may differ from a plain program's by a relative error of at most 0.0003.
Values sent between devices are 32-bit elements; how exact they have to be, the bound alone decides.
No kernel may reach another device: no remote copies, remote signals or barrier semaphores. Data moves between devices by JAX's collectives and lax.ppermute only.
A program may use at most 64 MiB of HBM per device.

v0:
```python
import jax
import jax.numpy as jnp
import numpy as np
from jax import lax
from jax.sharding import PartitionSpec as P

STEPS = 16


precise = lax.Precision.HIGHEST


def from_behind(value, axis, steps):
    count = lax.axis_size(axis)
    leading, last = (max(0, -steps), min(count, count - steps))
    return lax.ppermute(value, axis, [(source, source + steps) for source in range(leading, last)])


def rotate_pairs(entries, cos_part, sin_part, which_axis):
    middle = entries.shape[which_axis] // 2
    if which_axis == 1:
        leading = entries[:, :middle]
        trailing = entries[:, middle:]
        cos_row = cos_part[None, :]
        sin_row = sin_part[None, :]
        return jnp.concatenate(
            [cos_row * leading - sin_row * trailing, sin_row * leading + cos_row * trailing], axis=1
        )
    leading = entries[:middle]
    trailing = entries[middle:]
    cos_col = cos_part[:, None]
    sin_col = sin_part[:, None]
    return jnp.concatenate(
        [cos_col * leading - sin_col * trailing, sin_col * leading + cos_col * trailing], axis=0
    )


def reorder(entries, which_axis):
    middle = entries.shape[which_axis] // 2
    bounds = [
        (0, 1),
        (middle, middle + 1),
        (1, middle - 1),
        (middle + 1, 2 * middle),
        (middle - 1, middle),
    ]
    return jnp.concatenate(
        [
            lax.slice_in_dim(entries, first_at, last_at, axis=which_axis)
            for first_at, last_at in bounds
        ],
        axis=which_axis,
    )


def restore_table(order_size, step_count):
    labels = np.arange(order_size)
    middle = order_size // 2
    for number in range(step_count):
        labels = np.concatenate(
            [
                labels[0:1],
                labels[middle : middle + 1],
                labels[1 : middle - 1],
                labels[middle + 1 :],
                labels[middle - 1 : middle],
            ]
        )
    restore = np.argsort(labels)
    return np.eye(order_size, dtype=np.float32)[:, restore]


def jacobi_step(step_index, carried):
    products, rotation = carried
    middle = products.shape[0] // 2
    diagonal = jnp.diagonal(products)
    coupling = jnp.diagonal(products, offset=middle)
    angles = 0.5 * jnp.arctan2(-2.0 * coupling, diagonal[:middle] - diagonal[middle:])
    cos_part = jnp.cos(angles)
    sin_part = jnp.sin(angles)
    products = rotate_pairs(rotate_pairs(products, cos_part, sin_part, 1), cos_part, sin_part, 0)
    rotation = rotate_pairs(rotation, cos_part, sin_part, 1)
    return (reorder(reorder(products, 0), 1), reorder(rotation, 1))


def eigensolve(products):
    rotation = jnp.eye(products.shape[0], dtype=jnp.float32)
    products, rotation = lax.fori_loop(0, STEPS, jacobi_step, (products, rotation))
    table = jnp.asarray(restore_table(products.shape[0], STEPS), dtype=jnp.float32)
    return jnp.dot(rotation, table, precision=precise, preferred_element_type=jnp.float32)


def panel_product(left_panel, right_panel):
    return jnp.einsum(
        "ri,rj->ij", left_panel, right_panel, precision=precise, preferred_element_type=jnp.float32
    )


def project(panel, columns):
    return jnp.dot(panel, columns, precision=precise, preferred_element_type=jnp.float32)


def body(matrix):
    pair_count = lax.axis_size("pair")
    position = lax.axis_index("pair")
    middle = matrix.shape[1] // 2
    is_first = position == 0
    is_last = position == pair_count - 1
    first_gram = lax.psum(panel_product(matrix, matrix), "row")
    first_basis = eigensolve(first_gram)
    own_cols = first_basis[:, :middle]
    behind_cols = first_basis[:, middle:]
    own_bottom = project(matrix, behind_cols)
    from_later = from_behind(own_bottom, "pair", -1)
    own_top = project(matrix, own_cols)
    from_prior = from_behind(jnp.where(is_first, own_bottom, own_top), "pair", 1)
    upper_part = jnp.where(is_first, own_top, from_prior)
    lower_part = jnp.where(is_last, own_top, from_later)
    gram_upper = panel_product(upper_part, upper_part)
    gram_cross = panel_product(upper_part, lower_part)
    gram_lower = panel_product(lower_part, lower_part)
    local_gram = jnp.concatenate(
        [
            jnp.concatenate([gram_upper, gram_cross], axis=1),
            jnp.concatenate([gram_cross.T, gram_lower], axis=1),
        ],
        axis=0,
    )
    second_gram = lax.psum(local_gram, "row")
    second_basis = eigensolve(second_gram)
    rotated = project(upper_part, second_basis[:middle]) + project(
        lower_part, second_basis[middle:]
    )
    total_rows = matrix.shape[0] * lax.axis_size("row")
    energies = lax.psum(jnp.sum(rotated * rotated, axis=0), "row") / total_rows
    return (jnp.abs(rotated), energies)


def solution(mesh):
    return jax.shard_map(
        body,
        mesh=mesh,
        in_specs=(P("row", "pair"),),
        out_specs=(P("row", "pair"), P("pair")),
        check_vma=False,
    )
```

profile of v0, /device:TPU:121, one launch (start us, length us, event | category | flops | bytes accessed | tf_op | source)
XLA Modules:
  0.0 475.2 jit_solution(6762115386565713789)
XLA Ops:
  7.2 10.9 %fusion.24 = f32[256,256]{1,0:T(8,128)} fusion(f32[4096,256]{1,0:T(8,128)} %param.8), kind=kOutput, calls=%fused_computation.66 | convolution fusion | flops 3221225472 | bytes 4456448 | tf_op jit(solution)/shard_map/ri,rj->ij/dot_general | solution.py:94
  18.4 64.2 %all-reduce.3.cloned.1.call-done = f32[256,256]{1,0:T(8,128)} async-done(((f32[256,256]{1,0:T(8,128)}), f32[256,256]{1,0:T(8,128)}) %all-reduce.3.cloned.1.call-update) | async-done | bytes 262160 | tf_op jit(solution)/shard_map/psum | solution.py:109
  82.7 127.5 %while.24 = (s32[]{:T(128)}, f32[256,256]{1,0:T(8,128)}, f32[256,256]{1,0:T(8,128)S(1)}, s32[]{:T(128)}) while((s32[]{:T(128)}, f32[256,256]{1,0:T(8,128)}, f32[256,256]{1,0:T(8,128)S(1)}, s32[]{:T(128)}) %tuple.87), condition=%wide.region_2.4_spmd, body=%wide.region_1.3_spmd.sunk | while | flops 690690 | bytes 4729909 | solution.py:88
  84.8 2.6 gather_fusion
  92.8 2.6 gather_fusion
  100.8 2.6 gather_fusion
  108.7 2.6 gather_fusion
  116.7 2.6 gather_fusion
  124.7 2.6 gather_fusion
  132.6 2.6 gather_fusion
  140.6 2.6 gather_fusion
  148.6 2.6 gather_fusion
  156.5 2.6 gather_fusion
  164.5 2.6 gather_fusion
  172.5 2.6 gather_fusion
  180.4 2.6 gather_fusion
  188.4 2.6 gather_fusion
  196.4 2.6 gather_fusion
  204.3 2.6 gather_fusion
  210.6 6.9 %convolution_bitcast_fusion.1 = f32[4096,128]{0,1:T(8,128)S(1)} fusion(f32[4096,256]{1,0:T(8,128)} %param.8, f32[256,256]{1,0:T(8,128)S(1)} %fusion.25), kind=kOutput, calls=%fused_computation.44 | convolution fusion | flops 1610612736 | bytes 6422528 | tf_op jit(solution)/shard_map/dot_general | solution.py:100
  217.5 6.6 %broadcast_select_fusion.2 = (f32[4096,128]{0,1:T(8,128)}, f32[4096,128]{0,1:T(8,128)}) fusion(f32[4096,128]{0,1:T(8,128)S(1)} %convolution_bitcast_fusion.1, pred[]{:T(512)S(6)} %eq.12, f32[4096,256]{1,0:T(8,128)S(1)} %copy-done, f32[256,256]{1,0:T(8,128)S(1)} %fusion.25), kind=kOutput, calls=%fused_computation.48 | convolution fusion | flops 1611137024 | bytes 10616833 | tf_op jit(solution)/shard_map/dot_general | solution.py:100
  224.1 4.3 collective-permute-start
  230.6 40.3 %collective-permute-done = f32[4096,128]{0,1:T(8,128)S(1)} collective-permute-done((f32[4096,128]{0,1:T(8,128)}, f32[4096,128]{0,1:T(8,128)S(1)}, u32[]{:S(2)}, u32[]{:S(2)}) %collective-permute-start) | collective-permute-done | bytes 2097184 | tf_op jit(solution)/shard_map/ppermute | solution.py:16
  272.3 5.8 %collective-permute-done.1 = f32[4096,128]{0,1:T(8,128)} collective-permute-done((f32[4096,128]{0,1:T(8,128)}, f32[4096,128]{0,1:T(8,128)}, u32[]{:S(2)}, u32[]{:S(2)}) %collective-permute-start.1) | collective-permute-done | bytes 2097184 | tf_op jit(solution)/shard_map/ppermute | solution.py:16
  278.1 3.3 broadcast_select_fusion.1
  287.7 65.5 %all-reduce.5.cloned.1.call-done = f32[256,256]{0,1:T(8,128)} async-done(((f32[256,256]{0,1:T(8,128)}), f32[256,256]{0,1:T(8,128)}) %all-reduce.5.cloned.1.call-update) | async-done | bytes 262160 | tf_op jit(solution)/shard_map/psum | solution.py:129
  354.2 88.8 %while.25 = (s32[]{:T(128)}, f32[256,256]{1,0:T(8,128)S(1)}, f32[256,256]{1,0:T(8,128)S(1)}, s32[]{:T(128)}) while((s32[]{:T(128)}, f32[256,256]{1,0:T(8,128)S(1)}, f32[256,256]{1,0:T(8,128)S(1)}, s32[]{:T(128)}) %tuple.90), condition=%wide.region_5.7_spmd, body=%wide.region_4.6_spmd.sunk | while | flops 690690 | bytes 4729909 | solution.py:88
  356.0 2.3 gather_fusion.2
  361.6 2.3 gather_fusion.2
  444.4 3.6 fusion.11
  448.0 5.3 %multiply_reduce_fusion = (f32[256]{0:T(256)S(1)}, f32[4096,256]{1,0:T(8,128)}) fusion(f32[4096,256]{1,0:T(8,128)S(1)} %fusion.11, f32[4096,128]{0,1:T(8,128)S(1)} %copy-done.2, f32[256,256]{1,0:T(8,128)S(1)} %fusion.29), kind=kOutput, calls=%fused_computation.45 | convolution fusion | flops 1614806784 | bytes 10617856 | tf_op jit(solution)/shard_map/dot_general | solution.py:100
  453.3 14.5 %psum.23 = f32[256]{0:T(256)S(1)} all-reduce(f32[256]{0:T(256)S(1)} %get-tuple-element.91), channel_id=1, replica_groups=mesh['pair'=32,'row'=8] {'row'}, use_global_device_ids=true, to_apply=%region_7.9 | all-reduce | flops 256 | bytes 2048 | tf_op jit(solution)/shard_map/psum | solution.py:135
  (682 shorter events, 179.1 us)
Async XLA Ops:
  7.2 75.5 %all-reduce.3.cloned.1.call-start = ((), (), s32[]{:S(2)}) async-start(), calls=%async_computation | async-start | bytes 524288 | tf_op jit(solution)/shard_map/psum | solution.py:109
  18.2 335.0 %all-reduce.5.cloned.1.call-start = ((), (), s32[]{:S(2)}) async-start(), calls=%async_computation.1 | async-start | bytes 524288 | tf_op jit(solution)/shard_map/psum | solution.py:129
  82.7 127.5 %copy-start.5 = (f32[256,256]{1,0:T(8,128)S(1)}, f32[256,256]{1,0:T(8,128)}, u32[]{:S(2)}) copy-start(f32[256,256]{1,0:T(8,128)} %constant.49.clone) | copy-start | bytes 786436
  210.6 6.9 %copy-start = (f32[4096,256]{1,0:T(8,128)S(1)}, f32[4096,256]{1,0:T(8,128)}, u32[]{:S(2)}) copy-start(f32[4096,256]{1,0:T(8,128)} %param.8) | copy-start | bytes 12582916
  217.5 6.6 %copy-start.3 = (f32[4096,128]{0,1:T(8,128)}, f32[4096,128]{0,1:T(8,128)S(1)}, u32[]{:S(2)}) copy-start(f32[4096,128]{0,1:T(8,128)S(1)} %convolution_bitcast_fusion.1) | copy-start | bytes 6291460
  224.1 46.8 %collective-permute-start = (f32[4096,128]{0,1:T(8,128)}, f32[4096,128]{0,1:T(8,128)S(1)}, u32[]{:S(2)}, u32[]{:S(2)}) collective-permute-start(f32[4096,128]{0,1:T(8,128)} %get-tuple-element.95), channel_id=1, source_target_pairs={{0,8},{8,16},{16,24},{24,32},{32,40},{40,48},{48,56},{56,64},{64,7... | collective-permute-start | bytes 6291464 | tf_op jit(solution)/shard_map/ppermute | solution.py:16
  228.4 49.6 %collective-permute-start.1 = (f32[4096,128]{0,1:T(8,128)}, f32[4096,128]{0,1:T(8,128)}, u32[]{:S(2)}, u32[]{:S(2)}) collective-permute-start(f32[4096,128]{0,1:T(8,128)} %get-tuple-element.96), channel_id=1, source_target_pairs={{8,0},{16,8},{24,16},{32,24},{40,32},{48,40},{56,48},{64,56},{72,6... | collective-permute-start | bytes 6291464 | tf_op jit(solution)/shard_map/ppermute | solution.py:16
  270.9 1.4 copy-start.4
  281.3 1.8 copy-start.1
  444.4 3.6 copy-start.2
Sparse Core Ops, SparseCore 0:
  18.3 64.3 all-reduce.2
  287.8 65.3 all-reduce.4
where the time goes:
time: 479 us; the launch traced here: 475 us
  local copies, waits for them, and re-layouts  190 us (40%)
  waiting for transfers between devices  176 us (37%)
  matrix products  40.5 us (8%)
  other arithmetic  28.3 us (6%)
  blocking collectives  14.5 us (3%)
  between operations  14.2 us (3%)
  starting transfers between devices  6.71 us (1%)
  loops' own time  4.89 us (1%)
    gather x32, local copies, waits for them, and re-layouts, jacobi_step(): diagonal = jnp.diagonal(products)  78.6 us
    psum x1, waiting for transfers between devices, body(): second_gram = lax.psum(local_gram, 'row')  65.5 us
    psum x1, waiting for transfers between devices, body(): first_gram = lax.psum(panel_product(matrix, matrix), 'row')  64.2 us
    gather x32, local copies, waits for them, and re-layouts, jacobi_step(): coupling = jnp.diagonal(products, offset=middle)  56.8 us
    ppermute x2, waiting for transfers between devices, from_behind(): lax.ppermute(value, axis, [(source, source + steps) for source in range(l...  46.1 us
    concatenate x96, local copies, waits for them, and re-layouts, reorder(): jnp.concatenate([lax.slice_in_dim(entries, first_at, last_at, axis=which_...  31.9 us
    dot_general x4, matrix products, project(): jnp.dot(panel, columns, precision=precise, preferred_element_type=jnp.flo...  22.4 us
    slice x320, local copies, waits for them, and re-layouts, reorder(): lax.slice_in_dim(entries, first_at, last_at, axis=which_axis)  19.1 us
  transfers between devices with their start and end apart: 4, of which 4 were waited for; matrix products, arithmetic and copies ran while one was open for 0% of the time, Pallas kernels for 0%

commit v1 on v0

v1 whole, which is shorter than its diff:
```python
import jax
import jax.numpy as jnp
import numpy as np
from jax import lax
from jax.experimental import pallas as pl
from jax.experimental.pallas import tpu as pltpu
from jax.sharding import PartitionSpec as P

STEPS = 16
HALF = 128
PACKED = HALF + 8
CHUNK = 512
f32 = jnp.float32
bf16 = jnp.bfloat16


def restore_table(order_size, step_count):
    labels = np.arange(order_size)
    middle = order_size // 2
    for number in range(step_count):
        labels = np.concatenate(
            [
                labels[0:1],
                labels[middle : middle + 1],
                labels[1 : middle - 1],
                labels[middle + 1 :],
                labels[middle - 1 : middle],
            ]
        )
    restore = np.argsort(labels)
    return np.eye(order_size, dtype=np.float32)[:, restore]


def split(value):
    high = value.astype(bf16)
    return high, (value - high.astype(f32)).astype(bf16)


def dot(left, right):
    return jnp.dot(left, right, preferred_element_type=f32)


def dot_rows(left, right):
    return lax.dot_general(left, right, (((0,), (0,)), ((), ())), preferred_element_type=f32)


def diagonal_mask():
    across = lax.broadcasted_iota(jnp.int32, (HALF, HALF), 1)
    down = lax.broadcasted_iota(jnp.int32, (HALF, HALF), 0)
    return across, down


def pack(gram, core, mine_ref, other_ref):
    across, down = diagonal_mask()
    first = gram[:HALF, :HALF]
    second = gram[HALF:, HALF:]
    cross = gram[:HALF, HALF:]
    square = jnp.where(down <= across, first, second)
    diagonal = jnp.sum(jnp.where(down == across, second, 0.0), axis=0, keepdims=True)
    keeps_square = core == 0
    mine_ref[:HALF] = jnp.where(keeps_square, square, cross)
    other_ref[:HALF] = jnp.where(keeps_square, cross, square)
    strip = jnp.broadcast_to(diagonal, (8, HALF))
    mine_ref[HALF:] = strip
    other_ref[HALF:] = strip


def unpack(core, mine, other, lead_ref, trail_ref):
    across, down = diagonal_mask()
    keeps_square = core == 0
    square = jnp.where(keeps_square, mine[:HALF], other[:HALF])
    cross = jnp.where(keeps_square, other[:HALF], mine[:HALF])
    diagonal = jnp.where(keeps_square, mine[HALF : HALF + 1], other[HALF : HALF + 1])
    flipped = square.T
    lead_ref[:HALF] = jnp.where(down <= across, square, flipped)
    lead_ref[HALF:] = cross.T
    trail_ref[:HALF] = cross
    second = jnp.where(down > across, square, flipped)
    trail_ref[HALF:] = jnp.where(down == across, diagonal, second)


def first_gram_kernel(flags_ref, panel_ref, mine_ref, other_ref, same_ref, mixed_ref):
    at = pl.program_id(0)
    high, low = split(panel_ref[...])
    same = dot_rows(high, high)
    mixed = dot_rows(high, low)

    @pl.when(at == 0)
    def _():
        same_ref[...] = same
        mixed_ref[...] = mixed

    @pl.when(at > 0)
    def _():
        same_ref[...] += same
        mixed_ref[...] += mixed

    @pl.when(at == pl.num_programs(0) - 1)
    def _():
        mixed = mixed_ref[...]
        pack(same_ref[...] + (mixed + mixed.T), flags_ref[0], mine_ref, other_ref)


def second_gram_kernel(
    flags_ref, top_ref, upper_ref, lower_ref, mine_ref, other_ref, same_ref, mixed_ref
):
    at = pl.program_id(0)
    upper = jnp.where(flags_ref[1] == 1, top_ref[...], upper_ref[...])
    lower = jnp.where(flags_ref[2] == 1, top_ref[...], lower_ref[...])
    high, low = split(jnp.concatenate([upper, lower], axis=1))
    same = dot_rows(high, high)
    mixed = dot_rows(high, low)

    @pl.when(at == 0)
    def _():
        same_ref[...] = same
        mixed_ref[...] = mixed

    @pl.when(at > 0)
    def _():
        same_ref[...] += same
        mixed_ref[...] += mixed

    @pl.when(at == pl.num_programs(0) - 1)
    def _():
        mixed = mixed_ref[...]
        pack(same_ref[...] + (mixed + mixed.T), flags_ref[0], mine_ref, other_ref)


def gram_outputs():
    shape = jax.ShapeDtypeStruct((PACKED, HALF), f32)
    spec = pl.BlockSpec((PACKED, HALF), lambda i, flags: (0, 0))
    scratch = pltpu.VMEM((2 * HALF, 2 * HALF), f32)
    return (shape, shape), (spec, spec), [scratch, scratch]


def first_gram(flags, panel):
    shapes, specs, scratch = gram_outputs()
    return pl.pallas_call(
        first_gram_kernel,
        out_shape=shapes,
        grid_spec=pltpu.PrefetchScalarGridSpec(
            num_scalar_prefetch=1,
            grid=(panel.shape[0] // CHUNK,),
            in_specs=[pl.BlockSpec((CHUNK, 2 * HALF), lambda i, flags: (i, 0))],
            out_specs=specs,
            scratch_shapes=scratch,
        ),
    )(flags, panel)


def second_gram(flags, top, upper, lower):
    shapes, specs, scratch = gram_outputs()
    block = (CHUNK, HALF)
    return pl.pallas_call(
        second_gram_kernel,
        out_shape=shapes,
        grid_spec=pltpu.PrefetchScalarGridSpec(
            num_scalar_prefetch=1,
            grid=(top.shape[0] // CHUNK,),
            in_specs=[
                pl.BlockSpec(block, lambda i, flags: (i * (flags[1] + flags[2]), 0)),
                pl.BlockSpec(block, lambda i, flags: (i, 0)),
                pl.BlockSpec(block, lambda i, flags: (i, 0)),
            ],
            out_specs=specs,
            scratch_shapes=scratch,
        ),
    )(flags, top, upper, lower)


def turn(leading, trailing, cos_row, sin_row, across):
    first = cos_row * leading - sin_row * trailing
    second = sin_row * leading + cos_row * trailing
    moved = pltpu.roll(jnp.where(across == 0, second, first), 1, 1)
    top = jnp.where(across == 0, first, moved)
    bottom = jnp.where(across == HALF - 1, first, pltpu.roll(second, HALF - 1, 1))
    return top, bottom


def half_angle(first, coupling, second):
    along = first - second
    up = -2.0 * coupling
    along_size = jnp.abs(along)
    up_size = jnp.abs(up)
    scale = jnp.maximum(along_size, up_size)
    flat = scale == 0.0
    inverse = 1.0 / jnp.where(flat, 1.0, scale)
    along_part = jnp.where(flat, 1.0, along_size * inverse)
    up_part = up_size * inverse
    length = lax.rsqrt(along_part * along_part + up_part * up_part)
    square = 0.5 + 0.5 * (along_part * length)
    root = lax.rsqrt(square)
    large = square * root
    small = 0.5 * (up_part * length) * root
    ahead = along >= 0.0
    cos_part = jnp.where(ahead, large, small)
    sin_part = jnp.where(ahead, small, large)
    return cos_part, jnp.where(up > 0.0, sin_part, -sin_part)


def diagonal_of(square, mask):
    return jnp.sum(jnp.where(mask, square, 0.0), axis=0, keepdims=True)


def eigensolve(lead_ref, trail_ref, basis_lead_ref, basis_trail_ref):
    across = lax.broadcasted_iota(jnp.int32, (2 * HALF, HALF), 1)
    down = lax.broadcasted_iota(jnp.int32, (2 * HALF, HALF), 0)
    mask = (across == down)[:HALF]
    basis_lead_ref[...] = jnp.where(across == down, 1.0, 0.0)
    basis_trail_ref[...] = jnp.where(across + HALF == down, 1.0, 0.0)

    def step(number, carried):
        cos_row, sin_row = half_angle(
            diagonal_of(lead_ref[:HALF], mask),
            diagonal_of(trail_ref[:HALF], mask),
            diagonal_of(trail_ref[HALF:], mask),
        )
        lead, trail = turn(lead_ref[...], trail_ref[...], cos_row, sin_row, across)
        lead, trail = turn(
            jnp.concatenate([lead[:HALF].T, trail[:HALF].T], axis=0),
            jnp.concatenate([lead[HALF:].T, trail[HALF:].T], axis=0),
            cos_row,
            sin_row,
            across,
        )
        lead_ref[...] = lead
        trail_ref[...] = trail
        lead, trail = turn(basis_lead_ref[...], basis_trail_ref[...], cos_row, sin_row, across)
        basis_lead_ref[...] = lead
        basis_trail_ref[...] = trail
        return carried

    lax.fori_loop(0, STEPS, step, 0)


def restored(value, table):
    return jnp.dot(value, table, precision=lax.Precision.HIGHEST, preferred_element_type=f32)


def first_round_kernel(
    flags_ref,
    mine_ref,
    other_ref,
    table_ref,
    panel_hbm,
    down_hbm,
    up_hbm,
    top_hbm,
    panel_ref,
    down_ref,
    up_ref,
    top_ref,
    lead_ref,
    trail_ref,
    basis_lead_ref,
    basis_trail_ref,
    in_sem,
    down_sems,
    up_sems,
    top_sem,
):
    is_first = flags_ref[1] == 1
    at_edge = flags_ref[1] + flags_ref[2] > 0
    fetch = pltpu.make_async_copy(panel_hbm, panel_ref, in_sem)
    fetch.start()
    unpack(flags_ref[0], mine_ref[...], other_ref[...], lead_ref, trail_ref)
    eigensolve(lead_ref, trail_ref, basis_lead_ref, basis_trail_ref)
    basis = jnp.concatenate([basis_lead_ref[...], basis_trail_ref[...]], axis=1)
    basis_high, basis_low = split(restored(basis, table_ref[...]))
    fetch.wait()
    copies = []
    for number in range(panel_ref.shape[0] // CHUNK):
        rows = pl.ds(number * CHUNK, CHUNK)
        high, low = split(panel_ref[rows])
        product = dot(high, basis_high) + (dot(high, basis_low) + dot(low, basis_high))
        down_ref[rows] = product[:, HALF:]
        up_ref[rows] = jnp.where(is_first, product[:, HALF:], product[:, :HALF])
        top_ref[rows] = product[:, :HALF]
        for source, target, sems in (
            (down_ref, down_hbm, down_sems),
            (up_ref, up_hbm, up_sems),
        ):
            copy = pltpu.make_async_copy(source.at[rows], target.at[rows], sems.at[number])
            copy.start()
            copies.append(copy)

    @pl.when(at_edge)
    def _():
        copy = pltpu.make_async_copy(top_ref, top_hbm, top_sem)
        copy.start()
        copy.wait()

    for copy in copies:
        copy.wait()


def solve_scratch():
    return [pltpu.VMEM((2 * HALF, HALF), f32)] * 4


def first_round(flags, mine, other, table, panel):
    rows = panel.shape[0]
    shape = jax.ShapeDtypeStruct((rows, HALF), f32)
    count = rows // CHUNK
    anywhere = pl.BlockSpec(memory_space=pl.ANY)
    vmem = pl.BlockSpec(memory_space=pltpu.VMEM)
    return pl.pallas_call(
        first_round_kernel,
        out_shape=(shape, shape, shape),
        in_specs=[pl.BlockSpec(memory_space=pltpu.SMEM), vmem, vmem, vmem, anywhere],
        out_specs=(anywhere, anywhere, anywhere),
        scratch_shapes=[
            pltpu.VMEM((rows, 2 * HALF), f32),
            pltpu.VMEM((rows, HALF), f32),
            pltpu.VMEM((rows, HALF), f32),
            pltpu.VMEM((rows, HALF), f32),
        ]
        + solve_scratch()
        + [
            pltpu.SemaphoreType.DMA(()),
            pltpu.SemaphoreType.DMA((count,)),
            pltpu.SemaphoreType.DMA((count,)),
            pltpu.SemaphoreType.DMA(()),
        ],
        compiler_params=pltpu.CompilerParams(vmem_limit_bytes=32 * 2**20),
    )(flags, mine, other, table, panel)


def second_round_kernel(
    flags_ref,
    mine_ref,
    other_ref,
    table_ref,
    top_hbm,
    upper_hbm,
    lower_hbm,
    magnitudes_hbm,
    energies_ref,
    upper_ref,
    lower_ref,
    out_ref,
    lead_ref,
    trail_ref,
    basis_lead_ref,
    basis_trail_ref,
    in_sems,
    out_sems,
):
    is_first = flags_ref[1] == 1
    is_last = flags_ref[2] == 1

    def fetch(swapped, usual, target, sem):
        @pl.when(swapped)
        def _():
            pltpu.make_async_copy(top_hbm, target, sem).start()

        @pl.when(jnp.logical_not(swapped))
        def _():
            pltpu.make_async_copy(usual, target, sem).start()

    fetch(is_first, upper_hbm, upper_ref, in_sems.at[0])
    fetch(is_last, lower_hbm, lower_ref, in_sems.at[1])
    unpack(flags_ref[0], mine_ref[...], other_ref[...], lead_ref, trail_ref)
    eigensolve(lead_ref, trail_ref, basis_lead_ref, basis_trail_ref)
    table = table_ref[...]
    across, down = diagonal_mask()
    mask = across == down
    squares = jnp.concatenate(
        [diagonal_of(lead_ref[:HALF], mask), diagonal_of(trail_ref[HALF:], mask)], axis=1
    )
    squares = restored(jnp.broadcast_to(squares, (8, 2 * HALF)), table)
    energies_ref[...] = squares * (1.0 / (8 * upper_ref.shape[0]))
    basis = jnp.concatenate([basis_lead_ref[...], basis_trail_ref[...]], axis=1)
    basis_high, basis_low = split(restored(basis, table))
    pltpu.make_async_copy(upper_hbm, upper_ref, in_sems.at[0]).wait()
    pltpu.make_async_copy(lower_hbm, lower_ref, in_sems.at[1]).wait()
    copies = []
    for number in range(upper_ref.shape[0] // CHUNK):
        rows = pl.ds(number * CHUNK, CHUNK)
        high, low = split(jnp.concatenate([upper_ref[rows], lower_ref[rows]], axis=1))
        product = dot(high, basis_high) + (dot(high, basis_low) + dot(low, basis_high))
        out_ref[rows] = jnp.abs(product)
        copy = pltpu.make_async_copy(
            out_ref.at[rows], magnitudes_hbm.at[rows], out_sems.at[number]
        )
        copy.start()
        copies.append(copy)
    for copy in copies:
        copy.wait()


def second_round(flags, mine, other, table, top, upper, lower):
    rows = top.shape[0]
    count = rows // CHUNK
    anywhere = pl.BlockSpec(memory_space=pl.ANY)
    vmem = pl.BlockSpec(memory_space=pltpu.VMEM)
    return pl.pallas_call(
        second_round_kernel,
        out_shape=(
            jax.ShapeDtypeStruct((rows, 2 * HALF), f32),
            jax.ShapeDtypeStruct((8, 2 * HALF), f32),
        ),
        in_specs=[pl.BlockSpec(memory_space=pltpu.SMEM), vmem, vmem, vmem]
        + [anywhere, anywhere, anywhere],
        out_specs=(anywhere, vmem),
        scratch_shapes=[
            pltpu.VMEM((rows, HALF), f32),
            pltpu.VMEM((rows, HALF), f32),
            pltpu.VMEM((rows, 2 * HALF), f32),
        ]
        + solve_scratch()
        + [pltpu.SemaphoreType.DMA((2,)), pltpu.SemaphoreType.DMA((count,))],
        compiler_params=pltpu.CompilerParams(vmem_limit_bytes=32 * 2**20),
    )(flags, mine, other, table, top, upper, lower)


def row_sum(mine, other):
    count = lax.axis_size("row")
    swap = [(at, at ^ 1) for at in range(count)]

    def shifted(value, chips):
        return lax.ppermute(
            value, "row", [(at, (at + 2 * chips) % count) for at in range(count)]
        )

    part = mine + lax.ppermute(other, "row", swap)
    across = shifted(part, 2)
    ahead = shifted(part, 1)
    behind = shifted(part, -1)
    part = (part + across) + (ahead + behind)
    return part, lax.ppermute(part, "row", swap)


def from_behind(value, axis, steps):
    count = lax.axis_size(axis)
    leading, last = (max(0, -steps), min(count, count - steps))
    return lax.ppermute(value, axis, [(source, source + steps) for source in range(leading, last)])


def body(matrix):
    position = lax.axis_index("pair")
    is_first = position == 0
    is_last = position == lax.axis_size("pair") - 1
    core = lax.axis_index("row") % 2
    flags = jnp.stack([core, is_first, is_last]).astype(jnp.int32)
    table = jnp.asarray(restore_table(2 * HALF, STEPS))
    mine, other = row_sum(*first_gram(flags, matrix))
    down, up, top = first_round(flags, mine, other, table, matrix)
    lower = from_behind(down, "pair", -1)
    upper = from_behind(up, "pair", 1)
    mine, other = row_sum(*second_gram(flags, top, upper, lower))
    magnitudes, energies = second_round(flags, mine, other, table, top, upper, lower)
    return magnitudes, energies[0]


def solution(mesh):
    return jax.shard_map(
        body,
        mesh=mesh,
        in_specs=(P("row", "pair"),),
        out_specs=(P("row", "pair"), P("pair")),
        check_vma=False,
    )
```

time: 479 us -> 136 us (0.28)
  local copies, waits for them, and re-layouts: 190 us -> 8.57 us
  waiting for transfers between devices: 176 us -> 63.1 us
  Pallas kernels: 0 us -> 41.4 us
  matrix products: 40.5 us -> 0 us
  other arithmetic: 28.3 us -> 2.46 us
  blocking collectives: 14.5 us -> 0 us
  between operations: 14.2 us -> 0.71 us
  starting transfers between devices: 6.71 us -> 18.8 us
  loops' own time: 4.89 us -> 0 us
    gather x64 -> x0, local copies, waits for them, and re-layouts: 135 us -> none  [the longest x32 78.6 us: jacobi_step(): diagonal = jnp.diagonal(products)]
    psum x2 -> x0, waiting for transfers between devices: 130 us -> none  [the longest x1 65.5 us: body(): second_gram = lax.psum(local_gram, 'row')]
    pallas_call x0 -> x4, Pallas kernels: none -> 41.4 us  [the longest x1 13.6 us: first_round(): pl.pallas_call(first_round_kernel, out_shape=(shape, shape, shape), in_sp...]
    dot_general x10 -> x0, matrix products: 40.5 us -> none  [the longest x4 22.4 us: project(): jnp.dot(panel, columns, precision=precise, preferred_element_type=jnp.flo...]
    concatenate x96 -> x0, local copies, waits for them, and re-layouts: 31.9 us -> none  [reorder(): jnp.concatenate([lax.slice_in_dim(entries, first_at, last_at, axis=which_...]
    add x64 -> x4, other arithmetic: 20.7 us -> 1.82 us  [the longest x2 1.79 us: row_sum(): part = mine + lax.ppermute(other, 'row', swap)]
    slice x320 -> x1, local copies, waits for them, and re-layouts: 19.1 us -> 0.56 us  [body(): return (magnitudes, energies[0])]
    psum x1 -> x0, blocking collectives: 14.5 us -> none  [body(): energies = lax.psum(jnp.sum(rotated * rotated, axis=0), 'row') / total_rows]
  transfers between devices with their start and end apart: 4 -> 12, of which waited for: 4 -> 10; matrix products, arithmetic and copies ran while one was open for 0% -> 0% of each run, Pallas kernels for 0% -> 0%
where the time goes in v1:
time: 136 us; the launch traced here: 135 us
  waiting for transfers between devices  63.1 us (46%)
  Pallas kernels  41.4 us (30%)
  starting transfers between devices  18.8 us (14%)
  local copies, waits for them, and re-layouts  8.57 us (6%)
  other arithmetic  2.46 us (2%)
    ppermute x2, waiting for transfers between devices, from_behind(): lax.ppermute(value, axis, [(source, source + steps) for source in range(l...  49.8 us
    pallas_call x1, Pallas kernels, first_round(): pl.pallas_call(first_round_kernel, out_shape=(shape, shape, shape), in_sp...  13.6 us
    pallas_call x1, Pallas kernels, second_round(): pl.pallas_call(second_round_kernel, out_shape=(jax.ShapeDtypeStruct((rows...  12.2 us
    ppermute x6, waiting for transfers between devices, shifted(): lax.ppermute(value, 'row', [(at, (at + 2 * chips) % count) for at in rang...  9.2 us
    unnamed x20, local copies, waits for them, and re-layouts  8.01 us
    pallas_call x1, Pallas kernels, second_gram(): pl.pallas_call(second_gram_kernel, out_shape=shapes, grid_spec=pltpu.Pref...  7.89 us
    pallas_call x1, Pallas kernels, first_gram(): pl.pallas_call(first_gram_kernel, out_shape=shapes, grid_spec=pltpu.Prefe...  7.76 us
    ppermute x6, starting transfers between devices, shifted(): lax.ppermute(value, 'row', [(at, (at + 2 * chips) % count) for at in rang...  7.74 us
  transfers between devices with their start and end apart: 12, of which 10 were waited for; matrix products, arithmetic and copies ran while one was open for 0% of the time, Pallas kernels for 0%

profile of v1, /device:TPU:121, one launch (start us, length us, event | category | flops | bytes accessed | tf_op | source)
XLA Modules:
  0.0 135.1 jit_solution(15374237374668365729)
XLA Ops:
  0.6 0.6 pad_add_fusion.flags_ref
  1.3 7.8 %shard_map.41 = (f32[136,128]{1,0:T(8,128)}, f32[136,128]{1,0:T(8,128)}) custom-call(s32[3]{0:T(128)} %pad_add_fusion.flags_ref, f32[4096,256]{1,0:T(8,128)} %panel_hbm.1), custom_call_target="tpu_custom_call" | custom-call | tf_op jit(solution)/shard_map/pallas_call | solution.py:139
  9.0 0.7 collective-permute-start
  9.7 1.1 collective-permute-done
  10.8 0.9 add.29
  11.7 2.6 %collective-permute-start.3 = (f32[136,128]{1,0:T(8,128)S(1)}, f32[136,128]{1,0:T(8,128)S(1)}, u32[]{:S(2)}, u32[]{:S(2)}) collective-permute-start(f32[136,128]{1,0:T(8,128)S(1)} %add.29), channel_id=1, source_target_pairs={{0,6},{1,7},{2,0},{3,1},{4,2},{5,3},{6,4},{7,5},{8,14},{9,15},{10,... | collective-permute-start | bytes 208904 | tf_op jit(solution)/shard_map/ppermute | solution.py:423
  14.3 1.7 %collective-permute-start.1 = (f32[136,128]{1,0:T(8,128)S(1)}, f32[136,128]{1,0:T(8,128)S(1)}, u32[]{:S(2)}, u32[]{:S(2)}) collective-permute-start(f32[136,128]{1,0:T(8,128)S(1)} %add.29), channel_id=1, source_target_pairs={{0,4},{1,5},{2,6},{3,7},{4,0},{5,1},{6,2},{7,3},{8,12},{9,13},{10,... | collective-permute-start | bytes 208904 | tf_op jit(solution)/shard_map/ppermute | solution.py:423
  16.0 3.4 %collective-permute-done.2 = f32[136,128]{1,0:T(8,128)S(1)} collective-permute-done((f32[136,128]{1,0:T(8,128)S(1)}, f32[136,128]{1,0:T(8,128)S(1)}, u32[]{:S(2)}, u32[]{:S(2)}) %collective-permute-start.2) | collective-permute-done | bytes 69664 | tf_op jit(solution)/shard_map/ppermute | solution.py:423
  19.5 0.5 collective-permute-done.1
  20.0 1.7 %collective-permute-start.4 = (f32[136,128]{1,0:T(8,128)S(1)}, f32[136,128]{1,0:T(8,128)S(1)}, u32[]{:S(2)}, u32[]{:S(2)}) collective-permute-start(f32[136,128]{1,0:T(8,128)S(1)} %add_add_fusion.1.mine_ref), channel_id=1, source_target_pairs={{0,1},{1,0},{2,3},{3,2},{4,5},{5,4},{6,7},{7,6},{8,9},{9,8},{10,11... | collective-permute-start | bytes 208904 | tf_op jit(solution)/shard_map/ppermute | solution.py:432
  21.7 0.9 collective-permute-done.4.other_ref
  22.6 2.2 %copy-done = f32[4096,256]{1,0:T(8,128)S(1)} copy-done((f32[4096,256]{1,0:T(8,128)S(1)}, f32[4096,256]{1,0:T(8,128)}, u32[]{:S(2)}) %copy-start) | copy-done | bytes 4194328
  24.8 13.6 %shard_map.42 = (f32[4096,128]{1,0:T(8,128)S(1)}, f32[4096,128]{1,0:T(8,128)S(1)}, f32[4096,128]{1,0:T(8,128)S(1)}) custom-call(s32[3]{0:T(128)S(1)} %copy-done.8, f32[136,128]{1,0:T(8,128)S(1)} %add_add_fusion.1.mine_ref, f32[136,128]{1,0:T(8,128)S(1)} %collective-permute-done.4.other_ref, f32[256,256]{1,0:T(8,128)S(1)} %copy-done.7, f32[4096,256]{1,0:T(8,128)S(1)} %copy-done), custom_call_target="tpu_custom_call" | custom-call | tf_op jit(solution)/shard_map/pallas_call | solution.py:308
  38.4 1.3 copy-done.1
  39.7 4.4 %collective-permute-start.5 = (f32[4096,128]{1,0:T(8,128)S(1)}, f32[4096,128]{1,0:T(8,128)S(1)}, u32[]{:S(2)}, u32[]{:S(2)}) collective-permute-start(f32[4096,128]{1,0:T(8,128)S(1)} %get-tuple-element.14), channel_id=1, source_target_pairs={{0,8},{8,16},{16,24},{24,32},{32,40},{40,48},{48,56},{56,64},{64,7... | collective-permute-start | bytes 6291464 | tf_op jit(solution)/shard_map/ppermute | solution.py:438
  44.2 1.9 %collective-permute-start.6 = (f32[4096,128]{1,0:T(8,128)S(1)}, f32[4096,128]{1,0:T(8,128)S(1)}, u32[]{:S(2)}, u32[]{:S(2)}) collective-permute-start(f32[4096,128]{1,0:T(8,128)S(1)} %get-tuple-element.15), channel_id=1, source_target_pairs={{8,0},{16,8},{24,16},{32,24},{40,32},{48,40},{56,48},{64,56},{72,6... | collective-permute-start | bytes 6291464 | tf_op jit(solution)/shard_map/ppermute | solution.py:438
  46.1 42.7 %collective-permute-done.5.upper_ref.upper_hbm = f32[4096,128]{1,0:T(8,128)S(1)} collective-permute-done((f32[4096,128]{1,0:T(8,128)S(1)}, f32[4096,128]{1,0:T(8,128)S(1)}, u32[]{:S(2)}, u32[]{:S(2)}) %collective-permute-start.5) | collective-permute-done | bytes 2097184 | tf_op jit(solution)/shard_map/ppermute | solution.py:438
  88.8 7.1 %collective-permute-done.6.lower_ref.lower_hbm = f32[4096,128]{1,0:T(8,128)S(1)} collective-permute-done((f32[4096,128]{1,0:T(8,128)S(1)}, f32[4096,128]{1,0:T(8,128)S(1)}, u32[]{:S(2)}, u32[]{:S(2)}) %collective-permute-start.6) | collective-permute-done | bytes 2097184 | tf_op jit(solution)/shard_map/ppermute | solution.py:438
  95.9 1.3 copy-done.5
  97.2 7.9 %shard_map.43 = (f32[136,128]{1,0:T(8,128)}, f32[136,128]{1,0:T(8,128)}) custom-call(s32[3]{0:T(128)} %pad_add_fusion.flags_ref, f32[4096,128]{1,0:T(8,128)} %copy-done.1, f32[4096,128]{1,0:T(8,128)} %copy-done.3, f32[4096,128]{1,0:T(8,128)} %copy-done.5), custom_call_target="tpu_custom_call" | custom-call | tf_op jit(solution)/shard_map/pallas_call | solution.py:155
  105.1 1.5 %collective-permute-start.7 = (f32[136,128]{1,0:T(8,128)}, f32[136,128]{1,0:T(8,128)S(1)}, u32[]{:S(2)}, u32[]{:S(2)}) collective-permute-start(f32[136,128]{1,0:T(8,128)} %get-tuple-element.17), channel_id=1, source_target_pairs={{0,1},{1,0},{2,3},{3,2},{4,5},{5,4},{6,7},{7,6},{8,9},{9,8},{10,11... | collective-permute-start | bytes 208904 | tf_op jit(solution)/shard_map/ppermute | solution.py:427
  106.6 1.1 collective-permute-done.7
  107.7 0.9 add.33
  108.6 2.2 %collective-permute-start.10 = (f32[136,128]{1,0:T(8,128)S(1)}, f32[136,128]{1,0:T(8,128)S(1)}, u32[]{:S(2)}, u32[]{:S(2)}) collective-permute-start(f32[136,128]{1,0:T(8,128)S(1)} %add.33), channel_id=1, source_target_pairs={{0,6},{1,7},{2,0},{3,1},{4,2},{5,3},{6,4},{7,5},{8,14},{9,15},{10,... | collective-permute-start | bytes 208904 | tf_op jit(solution)/shard_map/ppermute | solution.py:423
  110.8 1.3 collective-permute-start.8
  112.2 5.1 %collective-permute-done.9 = f32[136,128]{1,0:T(8,128)S(1)} collective-permute-done((f32[136,128]{1,0:T(8,128)S(1)}, f32[136,128]{1,0:T(8,128)S(1)}, u32[]{:S(2)}, u32[]{:S(2)}) %collective-permute-start.9) | collective-permute-done | bytes 69664 | tf_op jit(solution)/shard_map/ppermute | solution.py:423
  117.3 0.9 collective-permute-start.11
  118.2 0.9 collective-permute-done.11.other_ref
  119.1 1.6 %copy-done.4 = f32[4096,128]{1,0:T(8,128)S(1)} copy-done((f32[4096,128]{1,0:T(8,128)S(1)}, f32[4096,128]{1,0:T(8,128)}, u32[]{:S(2)}) %copy-start.4) | copy-done | bytes 2097176
  120.7 1.6 %copy-done.6 = f32[4096,128]{1,0:T(8,128)S(1)} copy-done((f32[4096,128]{1,0:T(8,128)S(1)}, f32[4096,128]{1,0:T(8,128)}, u32[]{:S(2)}) %copy-start.6) | copy-done | bytes 2097176
  122.3 12.2 %shard_map.44 = (f32[4096,256]{1,0:T(8,128)}, f32[8,256]{1,0:T(8,128)S(1)}) custom-call(s32[3]{0:T(128)S(1)} %copy-done.9, f32[136,128]{1,0:T(8,128)S(1)} %add_add_fusion.mine_ref, f32[136,128]{1,0:T(8,128)S(1)} %collective-permute-done.11.other_ref, f32[256,256]{1,0:T(8,128)S(1)} %copy-done.7, f32[4096,128]{1,0:T(8,128)S(1)} %copy-done.2, ...), custom_call_target="tpu_custom_call" | custom-call | tf_op jit(solution)/shard_map/pallas_call | solution.py:398
  134.5 0.6 slice.3
  (22 shorter events, 0.2 us)
Async XLA Ops:
  1.3 21.3 %copy-start.7 = (f32[256,256]{1,0:T(8,128)S(1)}, f32[256,256]{1,0:T(8,128)}, u32[]{:S(2)}) copy-start(f32[256,256]{1,0:T(8,128)} %constant.27.clone.table_ref) | copy-start | bytes 786436
  1.3 21.3 %copy-start.8 = (s32[3]{0:T(128)S(1)}, s32[3]{0:T(128)}, u32[]{:S(2)}) copy-start(s32[3]{0:T(128)} %pad_add_fusion.flags_ref) | copy-start | bytes 40
  9.0 1.8 %collective-permute-start = (f32[136,128]{1,0:T(8,128)}, f32[136,128]{1,0:T(8,128)S(1)}, u32[]{:S(2)}, u32[]{:S(2)}) collective-permute-start(f32[136,128]{1,0:T(8,128)} %get-tuple-element.12), channel_id=1, source_target_pairs={{0,1},{1,0},{2,3},{3,2},{4,5},{5,4},{6,7},{7,6},{8,9},{9,8},{10,11... | collective-permute-start | bytes 208904 | tf_op jit(solution)/shard_map/ppermute | solution.py:427
  11.7 4.3 %collective-permute-start.3 = (f32[136,128]{1,0:T(8,128)S(1)}, f32[136,128]{1,0:T(8,128)S(1)}, u32[]{:S(2)}, u32[]{:S(2)}) collective-permute-start(f32[136,128]{1,0:T(8,128)S(1)} %add.29), channel_id=1, source_target_pairs={{0,6},{1,7},{2,0},{3,1},{4,2},{5,3},{6,4},{7,5},{8,14},{9,15},{10,... | collective-permute-start | bytes 208904 | tf_op jit(solution)/shard_map/ppermute | solution.py:423
  14.3 5.2 %collective-permute-start.2 = (f32[136,128]{1,0:T(8,128)S(1)}, f32[136,128]{1,0:T(8,128)S(1)}, u32[]{:S(2)}, u32[]{:S(2)}) collective-permute-start(f32[136,128]{1,0:T(8,128)S(1)} %add.29), channel_id=1, source_target_pairs={{0,2},{1,3},{2,4},{3,5},{4,6},{5,7},{6,0},{7,1},{8,10},{9,11},{10,... | collective-permute-start | bytes 208904 | tf_op jit(solution)/shard_map/ppermute | solution.py:423
  14.3 5.7 %collective-permute-start.1 = (f32[136,128]{1,0:T(8,128)S(1)}, f32[136,128]{1,0:T(8,128)S(1)}, u32[]{:S(2)}, u32[]{:S(2)}) collective-permute-start(f32[136,128]{1,0:T(8,128)S(1)} %add.29), channel_id=1, source_target_pairs={{0,4},{1,5},{2,6},{3,7},{4,0},{5,1},{6,2},{7,3},{8,12},{9,13},{10,... | collective-permute-start | bytes 208904 | tf_op jit(solution)/shard_map/ppermute | solution.py:423
  20.0 2.6 %collective-permute-start.4 = (f32[136,128]{1,0:T(8,128)S(1)}, f32[136,128]{1,0:T(8,128)S(1)}, u32[]{:S(2)}, u32[]{:S(2)}) collective-permute-start(f32[136,128]{1,0:T(8,128)S(1)} %add_add_fusion.1.mine_ref), channel_id=1, source_target_pairs={{0,1},{1,0},{2,3},{3,2},{4,5},{5,4},{6,7},{7,6},{8,9},{9,8},{10,11... | collective-permute-start | bytes 208904 | tf_op jit(solution)/shard_map/ppermute | solution.py:432
  22.6 2.2 %copy-start = (f32[4096,256]{1,0:T(8,128)S(1)}, f32[4096,256]{1,0:T(8,128)}, u32[]{:S(2)}) copy-start(f32[4096,256]{1,0:T(8,128)} %panel_hbm.1) | copy-start | bytes 12582916
  38.4 1.3 copy-start.1
  39.7 49.1 %collective-permute-start.5 = (f32[4096,128]{1,0:T(8,128)S(1)}, f32[4096,128]{1,0:T(8,128)S(1)}, u32[]{:S(2)}, u32[]{:S(2)}) collective-permute-start(f32[4096,128]{1,0:T(8,128)S(1)} %get-tuple-element.14), channel_id=1, source_target_pairs={{0,8},{8,16},{16,24},{24,32},{32,40},{40,48},{48,56},{56,64},{64,7... | collective-permute-start | bytes 6291464 | tf_op jit(solution)/shard_map/ppermute | solution.py:438
  44.2 51.8 %collective-permute-start.6 = (f32[4096,128]{1,0:T(8,128)S(1)}, f32[4096,128]{1,0:T(8,128)S(1)}, u32[]{:S(2)}, u32[]{:S(2)}) collective-permute-start(f32[4096,128]{1,0:T(8,128)S(1)} %get-tuple-element.15), channel_id=1, source_target_pairs={{8,0},{16,8},{24,16},{32,24},{40,32},{48,40},{56,48},{64,56},{72,6... | collective-permute-start | bytes 6291464 | tf_op jit(solution)/shard_map/ppermute | solution.py:438
  88.8 7.1 %copy-start.3 = (f32[4096,128]{1,0:T(8,128)}, f32[4096,128]{1,0:T(8,128)S(1)}, u32[]{:S(2)}) copy-start(f32[4096,128]{1,0:T(8,128)S(1)} %collective-permute-done.5.upper_ref.upper_hbm) | copy-start | bytes 6291460
  95.9 1.3 copy-start.5
  97.2 21.9 %copy-start.2 = (f32[4096,128]{1,0:T(8,128)S(1)}, f32[4096,128]{1,0:T(8,128)}, u32[]{:S(2)}) copy-start(f32[4096,128]{1,0:T(8,128)} %copy-done.1) | copy-start | bytes 6291460
  97.2 21.9 %copy-start.9 = (s32[3]{0:T(128)S(1)}, s32[3]{0:T(128)}, u32[]{:S(2)}) copy-start(s32[3]{0:T(128)} %pad_add_fusion.flags_ref) | copy-start | bytes 40
  105.1 2.6 %collective-permute-start.7 = (f32[136,128]{1,0:T(8,128)}, f32[136,128]{1,0:T(8,128)S(1)}, u32[]{:S(2)}, u32[]{:S(2)}) collective-permute-start(f32[136,128]{1,0:T(8,128)} %get-tuple-element.17), channel_id=1, source_target_pairs={{0,1},{1,0},{2,3},{3,2},{4,5},{5,4},{6,7},{7,6},{8,9},{9,8},{10,11... | collective-permute-start | bytes 208904 | tf_op jit(solution)/shard_map/ppermute | solution.py:427
  108.6 3.5 %collective-permute-start.10 = (f32[136,128]{1,0:T(8,128)S(1)}, f32[136,128]{1,0:T(8,128)S(1)}, u32[]{:S(2)}, u32[]{:S(2)}) collective-permute-start(f32[136,128]{1,0:T(8,128)S(1)} %add.33), channel_id=1, source_target_pairs={{0,6},{1,7},{2,0},{3,1},{4,2},{5,3},{6,4},{7,5},{8,14},{9,15},{10,... | collective-permute-start | bytes 208904 | tf_op jit(solution)/shard_map/ppermute | solution.py:423
  110.8 6.5 %collective-permute-start.9 = (f32[136,128]{1,0:T(8,128)S(1)}, f32[136,128]{1,0:T(8,128)S(1)}, u32[]{:S(2)}, u32[]{:S(2)}) collective-permute-start(f32[136,128]{1,0:T(8,128)S(1)} %add.33), channel_id=1, source_target_pairs={{0,2},{1,3},{2,4},{3,5},{4,6},{5,7},{6,0},{7,1},{8,10},{9,11},{10,... | collective-permute-start | bytes 208904 | tf_op jit(solution)/shard_map/ppermute | solution.py:423
  110.8 6.5 %collective-permute-start.8 = (f32[136,128]{1,0:T(8,128)S(1)}, f32[136,128]{1,0:T(8,128)S(1)}, u32[]{:S(2)}, u32[]{:S(2)}) collective-permute-start(f32[136,128]{1,0:T(8,128)S(1)} %add.33), channel_id=1, source_target_pairs={{0,4},{1,5},{2,6},{3,7},{4,0},{5,1},{6,2},{7,3},{8,12},{9,13},{10,... | collective-permute-start | bytes 208904 | tf_op jit(solution)/shard_map/ppermute | solution.py:423
  117.3 1.8 %collective-permute-start.11 = (f32[136,128]{1,0:T(8,128)S(1)}, f32[136,128]{1,0:T(8,128)S(1)}, u32[]{:S(2)}, u32[]{:S(2)}) collective-permute-start(f32[136,128]{1,0:T(8,128)S(1)} %add_add_fusion.mine_ref), channel_id=1, source_target_pairs={{0,1},{1,0},{2,3},{3,2},{4,5},{5,4},{6,7},{7,6},{8,9},{9,8},{10,11... | collective-permute-start | bytes 208904 | tf_op jit(solution)/shard_map/ppermute | solution.py:432
  119.1 1.6 %copy-start.4 = (f32[4096,128]{1,0:T(8,128)S(1)}, f32[4096,128]{1,0:T(8,128)}, u32[]{:S(2)}) copy-start(f32[4096,128]{1,0:T(8,128)} %copy-done.3) | copy-start | bytes 6291460
  120.7 1.6 %copy-start.6 = (f32[4096,128]{1,0:T(8,128)S(1)}, f32[4096,128]{1,0:T(8,128)}, u32[]{:S(2)}) copy-start(f32[4096,128]{1,0:T(8,128)} %copy-done.5) | copy-start | bytes 6291460

commit v2 on v0

v2 whole, which is shorter than its diff:
```python
import functools

import jax
import jax.numpy as jnp
import numpy as np
from jax import lax
from jax.experimental import pallas as pl
from jax.experimental.pallas import tpu as pltpu
from jax.sharding import PartitionSpec as P

STEPS = 16
HALF = 128
PACKED = HALF + 8
CHUNK = 512
CHUNKS = (2048, 1024, 1024)
f32 = jnp.float32
bf16 = jnp.bfloat16


def restore_table(order_size, step_count):
    labels = np.arange(order_size)
    middle = order_size // 2
    for number in range(step_count):
        labels = np.concatenate(
            [
                labels[0:1],
                labels[middle : middle + 1],
                labels[1 : middle - 1],
                labels[middle + 1 :],
                labels[middle - 1 : middle],
            ]
        )
    restore = np.argsort(labels)
    return np.eye(order_size, dtype=np.float32)[:, restore]


def split(value):
    high = value.astype(bf16)
    return high, (value - high.astype(f32)).astype(bf16)


def dot(left, right):
    return jnp.dot(left, right, preferred_element_type=f32)


def dot_rows(left, right):
    return lax.dot_general(left, right, (((0,), (0,)), ((), ())), preferred_element_type=f32)


def diagonal_mask():
    across = lax.broadcasted_iota(jnp.int32, (HALF, HALF), 1)
    down = lax.broadcasted_iota(jnp.int32, (HALF, HALF), 0)
    return across, down


def pack(gram, core, mine_ref, other_ref):
    across, down = diagonal_mask()
    first = gram[:HALF, :HALF]
    second = gram[HALF:, HALF:]
    cross = gram[:HALF, HALF:]
    square = jnp.where(down <= across, first, second)
    diagonal = jnp.sum(jnp.where(down == across, second, 0.0), axis=0, keepdims=True)
    keeps_square = core == 0
    mine_ref[:HALF] = jnp.where(keeps_square, square, cross)
    other_ref[:HALF] = jnp.where(keeps_square, cross, square)
    strip = jnp.broadcast_to(diagonal, (8, HALF))
    mine_ref[HALF:] = strip
    other_ref[HALF:] = strip


def unpack(core, mine, other, lead_ref, trail_ref):
    across, down = diagonal_mask()
    keeps_square = core == 0
    square = jnp.where(keeps_square, mine[:HALF], other[:HALF])
    cross = jnp.where(keeps_square, other[:HALF], mine[:HALF])
    diagonal = jnp.where(keeps_square, mine[HALF : HALF + 1], other[HALF : HALF + 1])
    flipped = square.T
    lead_ref[:HALF] = jnp.where(down <= across, square, flipped)
    lead_ref[HALF:] = cross.T
    trail_ref[:HALF] = cross
    second = jnp.where(down > across, square, flipped)
    trail_ref[HALF:] = jnp.where(down == across, diagonal, second)


def add_gram(total_ref, panel):
    high, low = split(panel)
    total_ref[...] += dot_rows(high, jnp.concatenate([high, low], axis=1))


def finish_gram(total_ref, mine_ref, other_ref):
    mixed = total_ref[:, 2 * HALF :]
    gram = total_ref[:, : 2 * HALF] + (mixed + mixed.T)
    pack(gram, lax.axis_index("row") % 2, mine_ref, other_ref)


def first_gram_kernel(panel_hbm, mine_ref, other_ref, panel_ref, total_ref, sems):
    copies = []
    for number in range(panel_hbm.shape[0] // CHUNK):
        rows = pl.ds(number * CHUNK, CHUNK)
        copy = pltpu.make_async_copy(panel_hbm.at[rows], panel_ref.at[rows], sems.at[number])
        copy.start()
        copies.append((rows, copy))
    total_ref[...] = jnp.zeros_like(total_ref)
    for rows, copy in copies:
        copy.wait()
        add_gram(total_ref, panel_ref[rows])
    finish_gram(total_ref, mine_ref, other_ref)


def second_panel(top_ref, upper_ref, lower_ref, rows):
    position = lax.axis_index("pair")
    top = top_ref[rows]
    upper = jnp.where(position == 0, top, upper_ref[rows])
    lower = jnp.where(position == lax.axis_size("pair") - 1, top, lower_ref[rows])
    return jnp.concatenate([upper, lower], axis=1)


def second_gram_kernel(is_first, is_last, *refs):
    before_ref = None
    if not is_first:
        before_ref, *refs = refs
    top_ref, upper_ref, lower_ref, *refs = refs
    if is_last:
        mine_ref, other_ref, *refs = refs
    (total_ref,) = refs
    if is_first:
        total_ref[...] = jnp.zeros_like(total_ref)
    else:
        total_ref[...] = before_ref[...]
    for number in range(upper_ref.shape[0] // CHUNK):
        rows = pl.ds(number * CHUNK, CHUNK)
        add_gram(total_ref, second_panel(top_ref, upper_ref, lower_ref, rows))
    if is_last:
        finish_gram(total_ref, mine_ref, other_ref)


VMEM = pltpu.VMEM
PACKED_PAIR = (VMEM((PACKED, HALF), f32),) * 2
TOTAL = VMEM((2 * HALF, 4 * HALF), f32)
IN_VMEM = pl.BlockSpec(memory_space=pltpu.VMEM)
IN_HBM = pl.BlockSpec(memory_space=pltpu.HBM)
DMA = pltpu.SemaphoreType.DMA


def in_vmem(*values):
    return [pltpu.with_memory_space_constraint(value, pltpu.VMEM) for value in values]


def in_hbm(value):
    return pltpu.with_memory_space_constraint(value, pltpu.HBM)


def params():
    return pltpu.CompilerParams(vmem_limit_bytes=16 * 2**20)


def cost(rows):
    return pl.CostEstimate(
        flops=2 * 3 * rows * 4 * HALF * HALF, bytes_accessed=16 * rows * HALF, transcendentals=0
    )


def first_gram(panel):
    rows = panel.shape[0]
    return pl.pallas_call(
        first_gram_kernel,
        out_shape=PACKED_PAIR + (VMEM(panel.shape, f32),),
        in_specs=[IN_HBM],
        out_specs=(IN_VMEM,) * 3,
        scratch_shapes=[TOTAL, DMA((rows // CHUNK,))],
        compiler_params=params(),
        cost_estimate=cost(rows),
    )(in_hbm(panel))


def second_gram(before, is_last, top, upper, lower):
    befores = [] if before is None else [before]
    operands = in_vmem(*befores, top, upper, lower)
    return pl.pallas_call(
        functools.partial(second_gram_kernel, before is None, is_last),
        out_shape=PACKED_PAIR if is_last else TOTAL,
        in_specs=[IN_VMEM] * len(operands),
        out_specs=(IN_VMEM, IN_VMEM) if is_last else IN_VMEM,
        scratch_shapes=[TOTAL] if is_last else [],
        compiler_params=params(),
        cost_estimate=cost(top.shape[0]),
    )(*operands)


def turn(leading, trailing, cos_row, sin_row, across):
    first = cos_row * leading - sin_row * trailing
    second = sin_row * leading + cos_row * trailing
    moved = pltpu.roll(jnp.where(across == 0, second, first), 1, 1)
    top = jnp.where(across == 0, first, moved)
    bottom = jnp.where(across == HALF - 1, first, pltpu.roll(second, HALF - 1, 1))
    return top, bottom


def half_angle(first, coupling, second):
    along = first - second
    up = -2.0 * coupling
    along_size = jnp.abs(along)
    up_size = jnp.abs(up)
    scale = jnp.maximum(along_size, up_size)
    flat = scale == 0.0
    inverse = 1.0 / jnp.where(flat, 1.0, scale)
    along_part = jnp.where(flat, 1.0, along_size * inverse)
    up_part = up_size * inverse
    length = lax.rsqrt(along_part * along_part + up_part * up_part)
    square = 0.5 + 0.5 * (along_part * length)
    root = lax.rsqrt(square)
    large = square * root
    small = 0.5 * (up_part * length) * root
    ahead = along >= 0.0
    cos_part = jnp.where(ahead, large, small)
    sin_part = jnp.where(ahead, small, large)
    return cos_part, jnp.where(up > 0.0, sin_part, -sin_part)


def eigensolve(lead_ref, trail_ref, basis_lead_ref, basis_trail_ref):
    across = lax.broadcasted_iota(jnp.int32, (2 * HALF, HALF), 1)
    down = lax.broadcasted_iota(jnp.int32, (2 * HALF, HALF), 0)
    mask = (across == down)[:HALF]
    basis_lead_ref[...] = jnp.where(across == down, 1.0, 0.0)
    basis_trail_ref[...] = jnp.where(across + HALF == down, 1.0, 0.0)

    def column_sums(value):
        return jnp.sum(value, axis=0, keepdims=True)

    def step(number, carried):
        cos_row, sin_row = half_angle(*carried)
        lead, trail = turn(lead_ref[...], trail_ref[...], cos_row, sin_row, across)
        lead_ref[...] = lead
        trail_ref[...] = trail
        basis_lead, basis_trail = turn(
            basis_lead_ref[...], basis_trail_ref[...], cos_row, sin_row, across
        )
        basis_lead_ref[...] = basis_lead
        basis_trail_ref[...] = basis_trail
        return (
            column_sums(basis_lead * lead),
            column_sums(basis_lead * trail),
            column_sums(basis_trail * trail),
        )

    def diagonal_of(square):
        return column_sums(jnp.where(mask, square, 0.0))

    first, _, second = lax.fori_loop(
        0,
        STEPS,
        step,
        (diagonal_of(lead_ref[:HALF]), diagonal_of(trail_ref[:HALF]), diagonal_of(trail_ref[HALF:])),
    )
    return jnp.concatenate([first, second], axis=1)


def restored_basis(basis_lead_ref, basis_trail_ref, table):
    basis = jnp.concatenate([basis_lead_ref[...], basis_trail_ref[...]], axis=1)
    high, low = split(basis)
    return dot(high, table).astype(bf16), dot(low, table).astype(bf16)


def product(panel, basis_high, basis_low):
    high, low = split(panel)
    return dot(high, basis_high) + (dot(high, basis_low) + dot(low, basis_high))


def first_round_kernel(mine_ref, other_ref, table_ref, panel_ref, *refs):
    outs, scratch = refs[: 3 * len(CHUNKS)], refs[3 * len(CHUNKS) :]
    unpack(lax.axis_index("row") % 2, mine_ref[...], other_ref[...], *scratch[:2])
    eigensolve(*scratch)
    basis = restored_basis(*scratch[2:], table_ref[...])
    is_first = lax.axis_index("pair") == 0
    start = 0
    for part, chunk in enumerate(CHUNKS):
        down_ref, up_ref, top_ref = outs[3 * part : 3 * part + 3]
        for number in range(chunk // CHUNK):
            rows = pl.ds(number * CHUNK, CHUNK)
            value = product(panel_ref[pl.ds(start + number * CHUNK, CHUNK)], *basis)
            down_ref[rows] = value[:, HALF:]
            up_ref[rows] = jnp.where(is_first, value[:, HALF:], value[:, :HALF])
            top_ref[rows] = value[:, :HALF]
        start += chunk


def solve_scratch():
    return [VMEM((2 * HALF, HALF), f32)] * 4


def first_round(mine, other, table, panel):
    return pl.pallas_call(
        first_round_kernel,
        out_shape=[VMEM((chunk, HALF), f32) for chunk in CHUNKS for _ in range(3)],
        in_specs=[IN_VMEM] * 4,
        out_specs=[IN_VMEM] * (3 * len(CHUNKS)),
        scratch_shapes=solve_scratch(),
        compiler_params=params(),
    )(*in_vmem(mine, other, table, panel))


def second_round_kernel(parts, *refs):
    mine_ref, other_ref, table_ref, *refs = refs
    sources, refs = refs[: 3 * parts], refs[3 * parts :]
    magnitudes_hbm, energies_ref, out_ref, *scratch, sems = refs
    unpack(lax.axis_index("row") % 2, mine_ref[...], other_ref[...], *scratch[:2])
    squares = eigensolve(*scratch)
    table = table_ref[...]
    basis = restored_basis(*scratch[2:], table)
    copies = []
    for part in range(parts):
        blocks = sources[3 * part : 3 * part + 3]
        for number in range(blocks[0].shape[0] // CHUNK):
            rows = pl.ds(len(copies) * CHUNK, CHUNK)
            panel = second_panel(*blocks, pl.ds(number * CHUNK, CHUNK))
            out_ref[rows] = jnp.abs(product(panel, *basis))
            copy = pltpu.make_async_copy(
                out_ref.at[rows], magnitudes_hbm.at[rows], sems.at[len(copies)]
            )
            copy.start()
            copies.append(copy)
    squares = jnp.dot(
        jnp.broadcast_to(squares, (8, 2 * HALF)),
        table.astype(f32),
        precision=lax.Precision.HIGHEST,
        preferred_element_type=f32,
    )
    total_rows = lax.axis_size("row") * out_ref.shape[0]
    energies_ref[...] = squares[:1] * (1.0 / total_rows)
    for copy in copies:
        copy.wait()


def second_round(mine, other, table, parts):
    rows = sum(part[0].shape[0] for part in parts)
    shape = (rows, 2 * HALF)
    operands = in_vmem(mine, other, table, *[value for part in parts for value in part])
    return pl.pallas_call(
        functools.partial(second_round_kernel, len(parts)),
        out_shape=(pltpu.HBM(shape, f32), jax.ShapeDtypeStruct((1, 2 * HALF), f32)),
        in_specs=[IN_VMEM] * len(operands),
        out_specs=(IN_HBM, IN_VMEM),
        scratch_shapes=[VMEM(shape, f32)] + solve_scratch() + [DMA((rows // CHUNK,))],
        compiler_params=params(),
    )(*operands)


def row_sum(mine, other):
    count = lax.axis_size("row")
    swap = [(at, at ^ 1) for at in range(count)]

    def shifted(value, chips):
        return lax.ppermute(
            value, "row", [(at, (at + 2 * chips) % count) for at in range(count)]
        )

    part = mine + lax.ppermute(other, "row", swap)
    across = shifted(part, 2)
    ahead = shifted(part, 1)
    behind = shifted(part, -1)
    part = (part + across) + (ahead + behind)
    return part, lax.ppermute(part, "row", swap)


def from_behind(value, axis, steps):
    count = lax.axis_size(axis)
    leading, last = (max(0, -steps), min(count, count - steps))
    return lax.ppermute(value, axis, [(source, source + steps) for source in range(leading, last)])


def body(matrix):
    table = jnp.asarray(restore_table(2 * HALF, STEPS), dtype=bf16)
    mine, other, panel = first_gram(matrix)
    blocks = first_round(*row_sum(mine, other), table, panel)
    parts = []
    for number in range(len(CHUNKS)):
        down, up, top = blocks[3 * number : 3 * number + 3]
        parts.append((top, from_behind(up, "pair", 1), from_behind(down, "pair", -1)))
    total = None
    for number, part in enumerate(parts):
        total = second_gram(total, number == len(parts) - 1, *part)
    magnitudes, energies = second_round(*row_sum(*total), table, parts)
    return magnitudes, energies.reshape(2 * HALF)


def solution(mesh):
    return jax.shard_map(
        body,
        mesh=mesh,
        in_specs=(P("row", "pair"),),
        out_specs=(P("row", "pair"), P("pair")),
        check_vma=False,
    )
```

time: 479 us -> 101 us (0.21)
  local copies, waits for them, and re-layouts: 190 us -> 0.01 us
  waiting for transfers between devices: 176 us -> 44 us
  matrix products: 40.5 us -> 0 us
  starting transfers between devices: 6.71 us -> 36.3 us
  other arithmetic: 28.3 us -> 0.05 us
  Pallas kernels: 0 us -> 19.3 us
  blocking collectives: 14.5 us -> 0 us
  between operations: 14.2 us -> 0.74 us
  loops' own time: 4.89 us -> 0 us
    gather x64 -> x0, local copies, waits for them, and re-layouts: 135 us -> none  [the longest x32 78.6 us: jacobi_step(): diagonal = jnp.diagonal(products)]
    psum x2 -> x0, waiting for transfers between devices: 130 us -> none  [the longest x1 65.5 us: body(): second_gram = lax.psum(local_gram, 'row')]
    dot_general x10 -> x0, matrix products: 40.5 us -> none  [the longest x4 22.4 us: project(): jnp.dot(panel, columns, precision=precise, preferred_element_type=jnp.flo...]
    concatenate x96 -> x0, local copies, waits for them, and re-layouts: 31.9 us -> none  [reorder(): jnp.concatenate([lax.slice_in_dim(entries, first_at, last_at, axis=which_...]
    add x64 -> x4, other arithmetic: 20.7 us -> 0.05 us  [the longest x2 0.03 us: row_sum(): part = part + across + (ahead + behind)]
    pallas_call x0 -> x6, Pallas kernels: none -> 19.3 us  [the longest x1 7.65 us: second_round(): pl.pallas_call(functools.partial(second_round_kernel, len(parts)), out_sh...]
    slice x320 -> x0, local copies, waits for them, and re-layouts: 19.1 us -> none  [reorder(): lax.slice_in_dim(entries, first_at, last_at, axis=which_axis)]
    ppermute x2 -> x6, starting transfers between devices: 6.45 us -> 23.7 us  [from_behind(): lax.ppermute(value, axis, [(source, source + steps) for source in range(l...]
  transfers between devices with their start and end apart: 4 -> 16, of which waited for: 4 -> 14; matrix products, arithmetic and copies ran while one was open for 0% -> 0% of each run, Pallas kernels for 0% -> 1%
where the time goes in v2:
time: 101 us; the launch traced here: 100 us
  waiting for transfers between devices  44 us (44%)
  starting transfers between devices  36.3 us (36%)
  Pallas kernels  19.3 us (19%)
    ppermute x6, waiting for transfers between devices, from_behind(): lax.ppermute(value, axis, [(source, source + steps) for source in range(l...  31.2 us
    ppermute x6, starting transfers between devices, from_behind(): lax.ppermute(value, axis, [(source, source + steps) for source in range(l...  23.7 us
    ppermute x6, waiting for transfers between devices, shifted(): lax.ppermute(value, 'row', [(at, (at + 2 * chips) % count) for at in rang...  9.19 us
    ppermute x6, starting transfers between devices, shifted(): lax.ppermute(value, 'row', [(at, (at + 2 * chips) % count) for at in rang...  7.73 us
    pallas_call x1, Pallas kernels, second_round(): pl.pallas_call(functools.partial(second_round_kernel, len(parts)), out_sh...  7.65 us
    pallas_call x1, Pallas kernels, first_round(): pl.pallas_call(first_round_kernel, out_shape=[VMEM((chunk, HALF), f32) fo...  6.02 us
    pallas_call x1, Pallas kernels, first_gram(): pl.pallas_call(first_gram_kernel, out_shape=PACKED_PAIR + (VMEM(panel.sha...  3.85 us
    ppermute x2, starting transfers between devices, row_sum(): return (part, lax.ppermute(part, 'row', swap))  2.58 us
  transfers between devices with their start and end apart: 16, of which 14 were waited for; matrix products, arithmetic and copies ran while one was open for 0% of the time, Pallas kernels for 1%

profile of v2, /device:TPU:121, one launch (start us, length us, event | category | flops | bytes accessed | tf_op | source)
XLA Modules:
  0.0 100.5 jit_solution(8491208715103379715)
XLA Ops:
  0.6 3.8 %shard_map.41 = (f32[136,128]{1,0:T(8,128)S(1)}, f32[136,128]{1,0:T(8,128)S(1)}, f32[4096,256]{1,0:T(8,128)S(1)}) custom-call(f32[4096,256]{1,0:T(8,128)} %panel_hbm.1), custom_call_target="tpu_custom_call" | custom-call | flops 1610612736 | bytes 8388608 | tf_op jit(solution)/shard_map/pallas_call | solution.py:165
  4.5 0.8 collective-permute-start
  5.3 0.9 collective-permute-done
  6.2 2.6 %collective-permute-start.3 = (f32[136,128]{1,0:T(8,128)S(1)}, f32[136,128]{1,0:T(8,128)S(1)}, u32[]{:S(2)}, u32[]{:S(2)}) collective-permute-start(f32[136,128]{1,0:T(8,128)S(1)} %add.24), channel_id=1, source_target_pairs={{0,6},{1,7},{2,0},{3,1},{4,2},{5,3},{6,4},{7,5},{8,14},{9,15},{10,... | collective-permute-start | bytes 208904 | tf_op jit(solution)/shard_map/ppermute | solution.py:353
  8.7 1.7 %collective-permute-start.1 = (f32[136,128]{1,0:T(8,128)S(1)}, f32[136,128]{1,0:T(8,128)S(1)}, u32[]{:S(2)}, u32[]{:S(2)}) collective-permute-start(f32[136,128]{1,0:T(8,128)S(1)} %add.24), channel_id=1, source_target_pairs={{0,4},{1,5},{2,6},{3,7},{4,0},{5,1},{6,2},{7,3},{8,12},{9,13},{10,... | collective-permute-start | bytes 208904 | tf_op jit(solution)/shard_map/ppermute | solution.py:353
  10.5 3.4 %collective-permute-done.2 = f32[136,128]{1,0:T(8,128)S(1)} collective-permute-done((f32[136,128]{1,0:T(8,128)S(1)}, f32[136,128]{1,0:T(8,128)S(1)}, u32[]{:S(2)}, u32[]{:S(2)}) %collective-permute-start.2) | collective-permute-done | bytes 69664 | tf_op jit(solution)/shard_map/ppermute | solution.py:353
  13.9 0.5 collective-permute-done.1
  14.5 1.7 %collective-permute-start.4 = (f32[136,128]{1,0:T(8,128)S(1)}, f32[136,128]{1,0:T(8,128)S(1)}, u32[]{:S(2)}, u32[]{:S(2)}) collective-permute-start(f32[136,128]{1,0:T(8,128)S(1)} %add_add_fusion.1.mine_ref), channel_id=1, source_target_pairs={{0,1},{1,0},{2,3},{3,2},{4,5},{5,4},{6,7},{7,6},{8,9},{9,8},{10,11... | collective-permute-start | bytes 208904 | tf_op jit(solution)/shard_map/ppermute | solution.py:362
  16.1 0.9 collective-permute-done.4.other_ref
  17.1 6.0 %shard_map.42 = (f32[2048,128]{1,0:T(8,128)S(1)}, f32[2048,128]{1,0:T(8,128)S(1)}, f32[2048,128]{1,0:T(8,128)S(1)}, f32[1024,128]{1,0:T(8,128)S(1)}, f32[1024,12...) custom-call(f32[136,128]{1,0:T(8,128)S(1)} %add_add_fusion.1.mine_re, ...), custom_call_target="tpu_custom_call" | custom-call | tf_op jit(solution)/shard_map/pallas_call | solution.py:292
  23.1 4.4 %collective-permute-start.5 = (f32[2048,128]{1,0:T(8,128)S(1)}, f32[2048,128]{1,0:T(8,128)S(1)}, u32[]{:S(2)}, u32[]{:S(2)}) collective-permute-start(f32[2048,128]{1,0:T(8,128)S(1)} %get-tuple-element.22), channel_id=1, source_target_pairs={{0,8},{8,16},{16,24},{24,32},{32,40},{40,48},{48,56},{56,64},{64,7... | collective-permute-start | bytes 3145736 | tf_op jit(solution)/shard_map/ppermute | solution.py:368
  27.5 1.9 %collective-permute-start.6 = (f32[2048,128]{1,0:T(8,128)S(1)}, f32[2048,128]{1,0:T(8,128)S(1)}, u32[]{:S(2)}, u32[]{:S(2)}) collective-permute-start(f32[2048,128]{1,0:T(8,128)S(1)} %get-tuple-element.23), channel_id=1, source_target_pairs={{8,0},{16,8},{24,16},{32,24},{40,32},{48,40},{56,48},{64,56},{72,6... | collective-permute-start | bytes 3145736 | tf_op jit(solution)/shard_map/ppermute | solution.py:368
  29.4 6.7 %collective-permute-start.7 = (f32[1024,128]{1,0:T(8,128)S(1)}, f32[1024,128]{1,0:T(8,128)S(1)}, u32[]{:S(2)}, u32[]{:S(2)}) collective-permute-start(f32[1024,128]{1,0:T(8,128)S(1)} %get-tuple-element.25), channel_id=1, source_target_pairs={{0,8},{8,16},{16,24},{24,32},{32,40},{40,48},{48,56},{56,64},{64,7... | collective-permute-start | bytes 1572872 | tf_op jit(solution)/shard_map/ppermute | solution.py:368
  36.1 1.9 %collective-permute-start.8 = (f32[1024,128]{1,0:T(8,128)S(1)}, f32[1024,128]{1,0:T(8,128)S(1)}, u32[]{:S(2)}, u32[]{:S(2)}) collective-permute-start(f32[1024,128]{1,0:T(8,128)S(1)} %get-tuple-element.26), channel_id=1, source_target_pairs={{8,0},{16,8},{24,16},{32,24},{40,32},{48,40},{56,48},{64,56},{72,6... | collective-permute-start | bytes 1572872 | tf_op jit(solution)/shard_map/ppermute | solution.py:368
  38.1 6.7 %collective-permute-start.9 = (f32[1024,128]{1,0:T(8,128)S(1)}, f32[1024,128]{1,0:T(8,128)S(1)}, u32[]{:S(2)}, u32[]{:S(2)}) collective-permute-start(f32[1024,128]{1,0:T(8,128)S(1)} %get-tuple-element.28), channel_id=1, source_target_pairs={{0,8},{8,16},{16,24},{24,32},{32,40},{40,48},{48,56},{56,64},{64,7... | collective-permute-start | bytes 1572872 | tf_op jit(solution)/shard_map/ppermute | solution.py:368
  44.7 4.9 %collective-permute-done.5.refs_1_.refs_4_ = f32[2048,128]{1,0:T(8,128)S(1)} collective-permute-done((f32[2048,128]{1,0:T(8,128)S(1)}, f32[2048,128]{1,0:T(8,128)S(1)}, u32[]{:S(2)}, u32[]{:S(2)}) %collective-permute-start.5) | collective-permute-done | bytes 1048608 | tf_op jit(solution)/shard_map/ppermute | solution.py:368
  49.7 2.0 %collective-permute-start.10 = (f32[1024,128]{1,0:T(8,128)S(1)}, f32[1024,128]{1,0:T(8,128)S(1)}, u32[]{:S(2)}, u32[]{:S(2)}) collective-permute-start(f32[1024,128]{1,0:T(8,128)S(1)} %get-tuple-element.29), channel_id=1, source_target_pairs={{8,0},{16,8},{24,16},{32,24},{40,32},{48,40},{56,48},{64,56},{72,6... | collective-permute-start | bytes 1572872 | tf_op jit(solution)/shard_map/ppermute | solution.py:368
  51.7 5.1 %collective-permute-done.6.refs_2_.refs_5_ = f32[2048,128]{1,0:T(8,128)S(1)} collective-permute-done((f32[2048,128]{1,0:T(8,128)S(1)}, f32[2048,128]{1,0:T(8,128)S(1)}, u32[]{:S(2)}, u32[]{:S(2)}) %collective-permute-start.6) | collective-permute-done | bytes 1048608 | tf_op jit(solution)/shard_map/ppermute | solution.py:368
  56.8 0.8 shard_map.43.refs_0_
  57.6 3.3 %collective-permute-done.7.refs_2_.refs_7_ = f32[1024,128]{1,0:T(8,128)S(1)} collective-permute-done((f32[1024,128]{1,0:T(8,128)S(1)}, f32[1024,128]{1,0:T(8,128)S(1)}, u32[]{:S(2)}, u32[]{:S(2)}) %collective-permute-start.7) | collective-permute-done | bytes 524320 | tf_op jit(solution)/shard_map/ppermute | solution.py:368
  60.9 7.1 %collective-permute-done.8.refs_3_.refs_8_ = f32[1024,128]{1,0:T(8,128)S(1)} collective-permute-done((f32[1024,128]{1,0:T(8,128)S(1)}, f32[1024,128]{1,0:T(8,128)S(1)}, u32[]{:S(2)}, u32[]{:S(2)}) %collective-permute-start.8) | collective-permute-done | bytes 524320 | tf_op jit(solution)/shard_map/ppermute | solution.py:368
  68.5 3.6 %collective-permute-done.9.refs_2_.refs_10_ = f32[1024,128]{1,0:T(8,128)S(1)} collective-permute-done((f32[1024,128]{1,0:T(8,128)S(1)}, f32[1024,128]{1,0:T(8,128)S(1)}, u32[]{:S(2)}, u32[]{:S(2)}) %collective-permute-start.9) | collective-permute-done | bytes 524320 | tf_op jit(solution)/shard_map/ppermute | solution.py:368
  72.1 7.1 %collective-permute-done.10.refs_3_.refs_11_ = f32[1024,128]{1,0:T(8,128)S(1)} collective-permute-done((f32[1024,128]{1,0:T(8,128)S(1)}, f32[1024,128]{1,0:T(8,128)S(1)}, u32[]{:S(2)}, u32[]{:S(2)}) %collective-permute-start.10) | collective-permute-done | bytes 524320 | tf_op jit(solution)/shard_map/ppermute | solution.py:368
  79.3 0.6 shard_map.45
  79.8 1.6 %collective-permute-start.11 = (f32[136,128]{1,0:T(8,128)S(1)}, f32[136,128]{1,0:T(8,128)S(1)}, u32[]{:S(2)}, u32[]{:S(2)}) collective-permute-start(f32[136,128]{1,0:T(8,128)S(1)} %get-tuple-element.31), channel_id=1, source_target_pairs={{0,1},{1,0},{2,3},{3,2},{4,5},{5,4},{6,7},{7,6},{8,9},{9,8},{10,11... | collective-permute-start | bytes 208904 | tf_op jit(solution)/shard_map/ppermute | solution.py:357
  81.4 0.9 collective-permute-done.11
  82.3 2.2 %collective-permute-start.14 = (f32[136,128]{1,0:T(8,128)S(1)}, f32[136,128]{1,0:T(8,128)S(1)}, u32[]{:S(2)}, u32[]{:S(2)}) collective-permute-start(f32[136,128]{1,0:T(8,128)S(1)} %add.28), channel_id=1, source_target_pairs={{0,6},{1,7},{2,0},{3,1},{4,2},{5,3},{6,4},{7,5},{8,14},{9,15},{10,... | collective-permute-start | bytes 208904 | tf_op jit(solution)/shard_map/ppermute | solution.py:353
  84.5 1.3 %collective-permute-start.12 = (f32[136,128]{1,0:T(8,128)S(1)}, f32[136,128]{1,0:T(8,128)S(1)}, u32[]{:S(2)}, u32[]{:S(2)}) collective-permute-start(f32[136,128]{1,0:T(8,128)S(1)} %add.28), channel_id=1, source_target_pairs={{0,4},{1,5},{2,6},{3,7},{4,0},{5,1},{6,2},{7,3},{8,12},{9,13},{10,... | collective-permute-start | bytes 208904 | tf_op jit(solution)/shard_map/ppermute | solution.py:353
  85.9 5.1 %collective-permute-done.13 = f32[136,128]{1,0:T(8,128)S(1)} collective-permute-done((f32[136,128]{1,0:T(8,128)S(1)}, f32[136,128]{1,0:T(8,128)S(1)}, u32[]{:S(2)}, u32[]{:S(2)}) %collective-permute-start.13) | collective-permute-done | bytes 69664 | tf_op jit(solution)/shard_map/ppermute | solution.py:353
  91.0 0.9 collective-permute-start.15
  91.9 0.9 collective-permute-done.15.refs_1_
  92.8 7.7 %shard_map.46 = (f32[4096,256]{1,0:T(8,128)}, f32[1,256]{1,0:T(1,128)}) custom-call(f32[136,128]{1,0:T(8,128)S(1)} %add_add_fusion.refs_0_, f32[136,128]{1,0:T(8,128)S(1)} %collective-permute-done.15.refs_1_, bf16[256,256]{1,0:T(8,128)(2,1)S(1)} %copy-done, f32[2048,128]{1,0:T(8,128)S(1)} %get-tuple-element.21.refs_0_.refs_3_, ...), custom_call_target="tpu_custom_call" | custom-call | tf_op jit(solution)/shard_map/pallas_call | solution.py:338
  (12 shorter events, 0.7 us)
Async XLA Ops:
  0.6 16.4 %copy-start = (bf16[256,256]{1,0:T(8,128)(2,1)S(1)}, bf16[256,256]{1,0:T(8,128)(2,1)}, u32[]{:S(2)}) copy-start(bf16[256,256]{1,0:T(8,128)(2,1)} %constant.2.clone.table_ref.refs_2_) | copy-start | bytes 393220
  4.5 1.7 %collective-permute-start = (f32[136,128]{1,0:T(8,128)S(1)}, f32[136,128]{1,0:T(8,128)S(1)}, u32[]{:S(2)}, u32[]{:S(2)}) collective-permute-start(f32[136,128]{1,0:T(8,128)S(1)} %get-tuple-element.19), channel_id=1, source_target_pairs={{0,1},{1,0},{2,3},{3,2},{4,5},{5,4},{6,7},{7,6},{8,9},{9,8},{10,11... | collective-permute-start | bytes 208904 | tf_op jit(solution)/shard_map/ppermute | solution.py:357
  6.2 4.3 %collective-permute-start.3 = (f32[136,128]{1,0:T(8,128)S(1)}, f32[136,128]{1,0:T(8,128)S(1)}, u32[]{:S(2)}, u32[]{:S(2)}) collective-permute-start(f32[136,128]{1,0:T(8,128)S(1)} %add.24), channel_id=1, source_target_pairs={{0,6},{1,7},{2,0},{3,1},{4,2},{5,3},{6,4},{7,5},{8,14},{9,15},{10,... | collective-permute-start | bytes 208904 | tf_op jit(solution)/shard_map/ppermute | solution.py:353
  8.7 5.2 %collective-permute-start.2 = (f32[136,128]{1,0:T(8,128)S(1)}, f32[136,128]{1,0:T(8,128)S(1)}, u32[]{:S(2)}, u32[]{:S(2)}) collective-permute-start(f32[136,128]{1,0:T(8,128)S(1)} %add.24), channel_id=1, source_target_pairs={{0,2},{1,3},{2,4},{3,5},{4,6},{5,7},{6,0},{7,1},{8,10},{9,11},{10,... | collective-permute-start | bytes 208904 | tf_op jit(solution)/shard_map/ppermute | solution.py:353
  8.7 5.7 %collective-permute-start.1 = (f32[136,128]{1,0:T(8,128)S(1)}, f32[136,128]{1,0:T(8,128)S(1)}, u32[]{:S(2)}, u32[]{:S(2)}) collective-permute-start(f32[136,128]{1,0:T(8,128)S(1)} %add.24), channel_id=1, source_target_pairs={{0,4},{1,5},{2,6},{3,7},{4,0},{5,1},{6,2},{7,3},{8,12},{9,13},{10,... | collective-permute-start | bytes 208904 | tf_op jit(solution)/shard_map/ppermute | solution.py:353
  14.5 2.6 %collective-permute-start.4 = (f32[136,128]{1,0:T(8,128)S(1)}, f32[136,128]{1,0:T(8,128)S(1)}, u32[]{:S(2)}, u32[]{:S(2)}) collective-permute-start(f32[136,128]{1,0:T(8,128)S(1)} %add_add_fusion.1.mine_ref), channel_id=1, source_target_pairs={{0,1},{1,0},{2,3},{3,2},{4,5},{5,4},{6,7},{7,6},{8,9},{9,8},{10,11... | collective-permute-start | bytes 208904 | tf_op jit(solution)/shard_map/ppermute | solution.py:362
  23.1 26.6 %collective-permute-start.5 = (f32[2048,128]{1,0:T(8,128)S(1)}, f32[2048,128]{1,0:T(8,128)S(1)}, u32[]{:S(2)}, u32[]{:S(2)}) collective-permute-start(f32[2048,128]{1,0:T(8,128)S(1)} %get-tuple-element.22), channel_id=1, source_target_pairs={{0,8},{8,16},{16,24},{24,32},{32,40},{40,48},{48,56},{56,64},{64,7... | collective-permute-start | bytes 3145736 | tf_op jit(solution)/shard_map/ppermute | solution.py:368
  27.5 29.3 %collective-permute-start.6 = (f32[2048,128]{1,0:T(8,128)S(1)}, f32[2048,128]{1,0:T(8,128)S(1)}, u32[]{:S(2)}, u32[]{:S(2)}) collective-permute-start(f32[2048,128]{1,0:T(8,128)S(1)} %get-tuple-element.23), channel_id=1, source_target_pairs={{8,0},{16,8},{24,16},{32,24},{40,32},{48,40},{56,48},{64,56},{72,6... | collective-permute-start | bytes 3145736 | tf_op jit(solution)/shard_map/ppermute | solution.py:368
  29.4 31.5 %collective-permute-start.7 = (f32[1024,128]{1,0:T(8,128)S(1)}, f32[1024,128]{1,0:T(8,128)S(1)}, u32[]{:S(2)}, u32[]{:S(2)}) collective-permute-start(f32[1024,128]{1,0:T(8,128)S(1)} %get-tuple-element.25), channel_id=1, source_target_pairs={{0,8},{8,16},{16,24},{24,32},{32,40},{40,48},{48,56},{56,64},{64,7... | collective-permute-start | bytes 1572872 | tf_op jit(solution)/shard_map/ppermute | solution.py:368
  36.1 31.9 %collective-permute-start.8 = (f32[1024,128]{1,0:T(8,128)S(1)}, f32[1024,128]{1,0:T(8,128)S(1)}, u32[]{:S(2)}, u32[]{:S(2)}) collective-permute-start(f32[1024,128]{1,0:T(8,128)S(1)} %get-tuple-element.26), channel_id=1, source_target_pairs={{8,0},{16,8},{24,16},{32,24},{40,32},{48,40},{56,48},{64,56},{72,6... | collective-permute-start | bytes 1572872 | tf_op jit(solution)/shard_map/ppermute | solution.py:368
  38.1 34.1 %collective-permute-start.9 = (f32[1024,128]{1,0:T(8,128)S(1)}, f32[1024,128]{1,0:T(8,128)S(1)}, u32[]{:S(2)}, u32[]{:S(2)}) collective-permute-start(f32[1024,128]{1,0:T(8,128)S(1)} %get-tuple-element.28), channel_id=1, source_target_pairs={{0,8},{8,16},{16,24},{24,32},{32,40},{40,48},{48,56},{56,64},{64,7... | collective-permute-start | bytes 1572872 | tf_op jit(solution)/shard_map/ppermute | solution.py:368
  49.7 29.6 %collective-permute-start.10 = (f32[1024,128]{1,0:T(8,128)S(1)}, f32[1024,128]{1,0:T(8,128)S(1)}, u32[]{:S(2)}, u32[]{:S(2)}) collective-permute-start(f32[1024,128]{1,0:T(8,128)S(1)} %get-tuple-element.29), channel_id=1, source_target_pairs={{8,0},{16,8},{24,16},{32,24},{40,32},{48,40},{56,48},{64,56},{72,6... | collective-permute-start | bytes 1572872 | tf_op jit(solution)/shard_map/ppermute | solution.py:368
  79.8 2.5 %collective-permute-start.11 = (f32[136,128]{1,0:T(8,128)S(1)}, f32[136,128]{1,0:T(8,128)S(1)}, u32[]{:S(2)}, u32[]{:S(2)}) collective-permute-start(f32[136,128]{1,0:T(8,128)S(1)} %get-tuple-element.31), channel_id=1, source_target_pairs={{0,1},{1,0},{2,3},{3,2},{4,5},{5,4},{6,7},{7,6},{8,9},{9,8},{10,11... | collective-permute-start | bytes 208904 | tf_op jit(solution)/shard_map/ppermute | solution.py:357
  82.3 3.5 %collective-permute-start.14 = (f32[136,128]{1,0:T(8,128)S(1)}, f32[136,128]{1,0:T(8,128)S(1)}, u32[]{:S(2)}, u32[]{:S(2)}) collective-permute-start(f32[136,128]{1,0:T(8,128)S(1)} %add.28), channel_id=1, source_target_pairs={{0,6},{1,7},{2,0},{3,1},{4,2},{5,3},{6,4},{7,5},{8,14},{9,15},{10,... | collective-permute-start | bytes 208904 | tf_op jit(solution)/shard_map/ppermute | solution.py:353
  84.5 6.5 %collective-permute-start.13 = (f32[136,128]{1,0:T(8,128)S(1)}, f32[136,128]{1,0:T(8,128)S(1)}, u32[]{:S(2)}, u32[]{:S(2)}) collective-permute-start(f32[136,128]{1,0:T(8,128)S(1)} %add.28), channel_id=1, source_target_pairs={{0,2},{1,3},{2,4},{3,5},{4,6},{5,7},{6,0},{7,1},{8,10},{9,11},{10,... | collective-permute-start | bytes 208904 | tf_op jit(solution)/shard_map/ppermute | solution.py:353
  84.5 6.5 %collective-permute-start.12 = (f32[136,128]{1,0:T(8,128)S(1)}, f32[136,128]{1,0:T(8,128)S(1)}, u32[]{:S(2)}, u32[]{:S(2)}) collective-permute-start(f32[136,128]{1,0:T(8,128)S(1)} %add.28), channel_id=1, source_target_pairs={{0,4},{1,5},{2,6},{3,7},{4,0},{5,1},{6,2},{7,3},{8,12},{9,13},{10,... | collective-permute-start | bytes 208904 | tf_op jit(solution)/shard_map/ppermute | solution.py:353
  91.0 1.8 %collective-permute-start.15 = (f32[136,128]{1,0:T(8,128)S(1)}, f32[136,128]{1,0:T(8,128)S(1)}, u32[]{:S(2)}, u32[]{:S(2)}) collective-permute-start(f32[136,128]{1,0:T(8,128)S(1)} %add_add_fusion.refs_0_), channel_id=1, source_target_pairs={{0,1},{1,0},{2,3},{3,2},{4,5},{5,4},{6,7},{7,6},{8,9},{9,8},{10,11... | collective-permute-start | bytes 208904 | tf_op jit(solution)/shard_map/ppermute | solution.py:362

commit v3 on v2

v3 whole, which is shorter than its diff:
```python
import functools

import jax
import jax.numpy as jnp
import numpy as np
from jax import lax
from jax.experimental import pallas as pl
from jax.experimental.pallas import tpu as pltpu
from jax.sharding import PartitionSpec as P

STEPS = 16
HALF = 128
REACH = 2 * STEPS - 1
CHUNK = 512
GRAM_CHUNK = 1024
CHUNKS = (2048, 1024, 1024)
f32 = jnp.float32
bf16 = jnp.bfloat16


def restore_table(order_size, step_count):
    labels = np.arange(order_size)
    middle = order_size // 2
    for number in range(step_count):
        labels = np.concatenate(
            [
                labels[0:1],
                labels[middle : middle + 1],
                labels[1 : middle - 1],
                labels[middle + 1 :],
                labels[middle - 1 : middle],
            ]
        )
    restore = np.argsort(labels)
    return np.eye(order_size, dtype=np.float32)[:, restore]


def split(value):
    high = value.astype(bf16)
    return high, (value - high.astype(f32)).astype(bf16)


def dot(left, right):
    return jnp.dot(left, right, preferred_element_type=f32)


def dot_rows(left, right):
    return lax.dot_general(left, right, (((0,), (0,)), ((), ())), preferred_element_type=f32)


def grid_of(rows):
    across = lax.broadcasted_iota(jnp.int32, (rows, HALF), 1)
    down = lax.broadcasted_iota(jnp.int32, (rows, HALF), 0)
    return across, down


def pack(gram, swapped, square_ref):
    first = jnp.where(swapped, gram[HALF:, HALF:], gram[:HALF, :HALF])
    second = jnp.where(swapped, gram[:HALF, :HALF], gram[HALF:, HALF:])
    cross = jnp.where(swapped, gram[HALF:, :HALF], gram[:HALF, HALF:])
    across, down = grid_of(HALF)
    ahead = (across - down) & (HALF - 1)
    square_ref[...] = jnp.where(
        jnp.logical_or(ahead < REACH, ahead > HALF - REACH),
        cross,
        jnp.where(
            ahead < 2 * REACH, pltpu.roll(first, REACH, 1), pltpu.roll(second, 2 * REACH, 1)
        ),
    )


def fold(value):
    return value[: HALF // 2] + value[HALF // 2 :]


def unfold(value):
    across, down = grid_of(HALF)
    near = jnp.abs(across - down) < HALF // 4
    return jnp.where(near, jnp.concatenate([value, value], axis=0), 0.0)


def unpack(square, lead_ref, trail_ref):
    across, down = grid_of(HALF)
    ahead = across - down

    def symmetric(moved):
        upper = pltpu.roll(square, HALF - moved, 1)
        upper = jnp.where(jnp.logical_and(ahead >= 0, ahead < REACH), upper, 0.0)
        return fold(jnp.where(ahead >= 0, upper, upper.T))

    cross = jnp.where(jnp.abs(ahead) < REACH, square, 0.0)
    lead_ref[: HALF // 2] = symmetric(REACH)
    lead_ref[HALF // 2 :] = fold(cross.T)
    trail_ref[: HALF // 2] = fold(cross)
    trail_ref[HALF // 2 :] = symmetric(2 * REACH)


def add_gram(total_ref, panel):
    high, low = split(panel)
    total_ref[...] += dot_rows(high, jnp.concatenate([high, low], axis=1))


def finish_gram(total_ref, swapped, square_ref):
    mixed = total_ref[:, 2 * HALF :]
    gram = total_ref[:, : 2 * HALF] + (mixed + mixed.T)
    pack(gram, swapped, square_ref)


def first_gram_kernel(panel_hbm, square_ref, panel_ref, total_ref, sems):
    copies = []
    for number in range(panel_hbm.shape[0] // GRAM_CHUNK):
        rows = pl.ds(number * GRAM_CHUNK, GRAM_CHUNK)
        copy = pltpu.make_async_copy(panel_hbm.at[rows], panel_ref.at[rows], sems.at[number])
        copy.start()
        copies.append((rows, copy))
    total_ref[...] = jnp.zeros_like(total_ref)
    for rows, copy in copies:
        copy.wait()
        add_gram(total_ref, panel_ref[rows])
    finish_gram(total_ref, False, square_ref)


def is_odd():
    return lax.axis_index("pair") % 2 == 1


def second_gram_kernel(is_first, is_last, *refs):
    before_ref = None
    if not is_first:
        before_ref, *refs = refs
    far_ref, near_ref, *refs = refs
    if is_last:
        square_ref, *refs = refs
    (total_ref,) = refs
    if is_first:
        total_ref[...] = jnp.zeros_like(total_ref)
    else:
        total_ref[...] = before_ref[...]
    for number in range(near_ref.shape[0] // GRAM_CHUNK):
        rows = pl.ds(number * GRAM_CHUNK, GRAM_CHUNK)
        add_gram(total_ref, jnp.concatenate([far_ref[rows], near_ref[rows]], axis=1))
    if is_last:
        finish_gram(total_ref, is_odd(), square_ref)


VMEM = pltpu.VMEM
SQUARE = VMEM((HALF, HALF), f32)
TOTAL = VMEM((2 * HALF, 4 * HALF), f32)
IN_VMEM = pl.BlockSpec(memory_space=pltpu.VMEM)
IN_HBM = pl.BlockSpec(memory_space=pltpu.HBM)
DMA = pltpu.SemaphoreType.DMA


def in_vmem(*values):
    return [pltpu.with_memory_space_constraint(value, pltpu.VMEM) for value in values]


def in_hbm(value):
    return pltpu.with_memory_space_constraint(value, pltpu.HBM)


def params():
    return pltpu.CompilerParams(vmem_limit_bytes=16 * 2**20)


def cost(rows):
    return pl.CostEstimate(
        flops=2 * 3 * rows * 4 * HALF * HALF, bytes_accessed=16 * rows * HALF, transcendentals=0
    )


def first_gram(panel):
    rows = panel.shape[0]
    return pl.pallas_call(
        first_gram_kernel,
        out_shape=(SQUARE, VMEM(panel.shape, f32)),
        in_specs=[IN_HBM],
        out_specs=(IN_VMEM, IN_VMEM),
        scratch_shapes=[TOTAL, DMA((rows // GRAM_CHUNK,))],
        compiler_params=params(),
        cost_estimate=cost(rows),
    )(in_hbm(panel))


def second_gram(before, is_last, far, near):
    befores = [] if before is None else [before]
    operands = in_vmem(*befores, far, near)
    return pl.pallas_call(
        functools.partial(second_gram_kernel, before is None, is_last),
        out_shape=SQUARE if is_last else TOTAL,
        in_specs=[IN_VMEM] * len(operands),
        out_specs=IN_VMEM,
        scratch_shapes=[TOTAL] if is_last else [],
        compiler_params=params(),
        cost_estimate=cost(near.shape[0]),
    )(*operands)


def rotate(leading, trailing, cos_row, sin_row):
    return cos_row * leading - sin_row * trailing, sin_row * leading + cos_row * trailing


def move(first, second, across):
    moved = pltpu.roll(jnp.where(across == 0, second, first), 1, 1)
    top = jnp.where(across == 0, first, moved)
    bottom = jnp.where(across == HALF - 1, first, pltpu.roll(second, HALF - 1, 1))
    return top, bottom


def half_angle(first, coupling, second):
    along = first - second
    up = -2.0 * coupling
    along_size = jnp.abs(along)
    up_size = jnp.abs(up)
    scale = jnp.maximum(along_size, up_size)
    flat = scale == 0.0
    inverse = 1.0 / jnp.where(flat, 1.0, scale)
    along_part = jnp.where(flat, 1.0, along_size * inverse)
    up_part = up_size * inverse
    length = lax.rsqrt(along_part * along_part + up_part * up_part)
    square = 0.5 + 0.5 * (along_part * length)
    root = lax.rsqrt(square)
    large = square * root
    small = 0.5 * (up_part * length) * root
    ahead = along >= 0.0
    cos_part = jnp.where(ahead, large, small)
    sin_part = jnp.where(ahead, small, large)
    return cos_part, jnp.where(up > 0.0, sin_part, -sin_part)


def eigensolve(lead_ref, trail_ref, basis_lead_ref, basis_trail_ref):
    across, down = grid_of(HALF)
    half = HALF // 2
    mask = jnp.logical_and((across & (half - 1)) == (down & (half - 1)), down < half)
    basis_lead_ref[...] = jnp.where(mask, 1.0, 0.0)
    basis_trail_ref[...] = jnp.where(
        jnp.logical_and((across & (half - 1)) == (down & (half - 1)), down >= half), 1.0, 0.0
    )

    def column_sums(value):
        return jnp.sum(value, axis=0, keepdims=True)

    def step(number, carried):
        turns = half_angle(*carried)
        product = rotate(lead_ref[...], trail_ref[...], *turns)
        basis = rotate(basis_lead_ref[...], basis_trail_ref[...], *turns)
        first, second = move(
            column_sums(product[0] * basis[0]), column_sums(product[1] * basis[1]), across[:1]
        )
        lead_ref[...], trail = move(*product, across)
        trail_ref[...] = trail
        basis_lead, basis_trail_ref[...] = move(*basis, across)
        basis_lead_ref[...] = basis_lead
        return first, column_sums(basis_lead * trail), second

    def diagonal_of(folded):
        return column_sums(jnp.where(mask[:half], folded, 0.0))

    first, _, second = lax.fori_loop(
        0,
        STEPS,
        step,
        (diagonal_of(lead_ref[:half]), diagonal_of(trail_ref[:half]), diagonal_of(trail_ref[half:])),
        unroll=4,
    )
    return jnp.concatenate([first, second], axis=1)


def restored_basis(basis_lead_ref, basis_trail_ref, table):
    half = HALF // 2
    basis = jnp.concatenate(
        [
            jnp.concatenate([unfold(ref[:half]), unfold(ref[half:])], axis=0)
            for ref in (basis_lead_ref, basis_trail_ref)
        ],
        axis=1,
    )
    high, low = split(basis)
    return dot(high, table).astype(bf16), dot(low, table).astype(bf16)


def product(panel, basis_high, basis_low):
    high, low = split(panel)
    return dot(high, basis_high) + (dot(high, basis_low) + dot(low, basis_high))


def project(panel_ref, basis, start, near_ref, far_ref):
    for number in range(near_ref.shape[0] // CHUNK):
        rows = pl.ds(number * CHUNK, CHUNK)
        value = product(panel_ref[pl.ds(start + number * CHUNK, CHUNK)], *basis)
        near_ref[rows] = value[:, :HALF]
        far_ref[rows] = value[:, HALF:]


def first_round_kernel(
    *refs,
):
    *parts, table_ref, panel_ref, near_ref, far_ref, high_ref, low_ref = refs[:10]
    scratch = refs[10:]
    unpack(total_of(parts), *scratch[:2])
    eigensolve(*scratch)
    swapped = jnp.logical_or(lax.axis_index("pair") == 0, is_odd())
    basis = [
        jnp.where(swapped, jnp.concatenate([value[:, HALF:], value[:, :HALF]], axis=1), value)
        for value in restored_basis(*scratch[2:], table_ref[...])
    ]
    project(panel_ref, basis, 0, near_ref, far_ref)
    high_ref[...], low_ref[...] = basis


def later_rows_kernel(high_ref, low_ref, panel_ref, *outs):
    start = CHUNKS[0]
    for part in range(0, len(outs), 2):
        project(panel_ref, (high_ref[...], low_ref[...]), start, *outs[part : part + 2])
        start += outs[part].shape[0]


def solve_scratch():
    return [VMEM((HALF, HALF), f32)] * 4


def first_round(sums, table, panel):
    basis = VMEM((2 * HALF, 2 * HALF), bf16)
    near, far, high, low = pl.pallas_call(
        first_round_kernel,
        out_shape=[VMEM((CHUNKS[0], HALF), f32)] * 2 + [basis] * 2,
        in_specs=[IN_VMEM] * 6,
        out_specs=[IN_VMEM] * 4,
        scratch_shapes=solve_scratch(),
        compiler_params=params(),
    )(*in_vmem(*sums, table, panel))
    later = pl.pallas_call(
        later_rows_kernel,
        out_shape=[VMEM((chunk, HALF), f32) for chunk in CHUNKS[1:] for _ in range(2)],
        in_specs=[IN_VMEM] * 3,
        out_specs=[IN_VMEM] * (2 * len(CHUNKS) - 2),
        compiler_params=params(),
        cost_estimate=cost(sum(CHUNKS[1:])),
    )(*in_vmem(high, low, panel))
    return [near, far] + list(later)


def second_round_kernel(parts, *refs):
    parts_of_sum, (table_ref, *refs) = refs[:4], refs[4:]
    sources, refs = refs[: 2 * parts], refs[2 * parts :]
    magnitudes_hbm, energies_ref, out_ref, *scratch, sems = refs
    unpack(total_of(parts_of_sum), *scratch[:2])
    squares = eigensolve(*scratch)
    table = table_ref[...]
    basis = [
        jnp.where(is_odd(), jnp.concatenate([value[HALF:], value[:HALF]], axis=0), value)
        for value in restored_basis(*scratch[2:], table)
    ]
    copies = []
    for part in range(parts):
        far_ref, near_ref = sources[2 * part : 2 * part + 2]
        for number in range(near_ref.shape[0] // CHUNK):
            rows = pl.ds(len(copies) * CHUNK, CHUNK)
            source = pl.ds(number * CHUNK, CHUNK)
            panel = jnp.concatenate([far_ref[source], near_ref[source]], axis=1)
            out_ref[rows] = jnp.abs(product(panel, *basis))
            copy = pltpu.make_async_copy(
                out_ref.at[rows], magnitudes_hbm.at[rows], sems.at[len(copies)]
            )
            copy.start()
            copies.append(copy)
    squares = jnp.dot(
        jnp.broadcast_to(squares, (8, 2 * HALF)),
        table.astype(f32),
        precision=lax.Precision.HIGHEST,
        preferred_element_type=f32,
    )
    total_rows = lax.axis_size("row") * out_ref.shape[0]
    energies_ref[...] = squares[:1] * (1.0 / total_rows)
    for copy in copies:
        copy.wait()


def second_round(sums, table, parts):
    rows = sum(part[0].shape[0] for part in parts)
    shape = (rows, 2 * HALF)
    operands = in_vmem(*sums, table, *[value for part in parts for value in part])
    return pl.pallas_call(
        functools.partial(second_round_kernel, len(parts)),
        out_shape=(pltpu.HBM(shape, f32), jax.ShapeDtypeStruct((1, 2 * HALF), f32)),
        in_specs=[IN_VMEM] * len(operands),
        out_specs=(IN_HBM, IN_VMEM),
        scratch_shapes=[VMEM(shape, f32)] + solve_scratch() + [DMA((rows // CHUNK,))],
        compiler_params=params(),
    )(*operands)


def row_sum(square):
    count = lax.axis_size("row")

    def shifted(value, chips):
        return lax.ppermute(value, "row", [(at, (at + 2 * chips) % count) for at in range(count)])

    square = square + lax.ppermute(square, "row", [(at, at ^ 1) for at in range(count)])
    return shifted(square, 1), shifted(square, -1), square, shifted(square, 2)


def total_of(parts):
    ahead, behind, own, across = [part[...] for part in parts]
    return (ahead + behind) + (own + across)


def exchange(near, far):
    last = lax.axis_size("pair") - 1
    inner = [(at, at - 1 + 2 * (at % 2)) for at in range(1, last)]
    return (
        lax.ppermute(far, "pair", [(0, 0)] + inner + [(last, last)]),
        lax.ppermute(near, "pair", [(at, at ^ 1) for at in range(last + 1)]),
    )


def body(matrix):
    table = jnp.asarray(restore_table(2 * HALF, STEPS), dtype=bf16)
    square, panel = first_gram(matrix)
    blocks = first_round(row_sum(square), table, panel)
    parts = [exchange(*blocks[at : at + 2]) for at in range(0, len(blocks), 2)]
    total = None
    for number, part in enumerate(parts):
        total = second_gram(total, number == len(parts) - 1, *part)
    magnitudes, energies = second_round(row_sum(total), table, parts)
    return magnitudes, energies.reshape(2 * HALF)


def solution(mesh):
    return jax.shard_map(
        body,
        mesh=mesh,
        in_specs=(P("row", "pair"),),
        out_specs=(P("row", "pair"), P("pair")),
        check_vma=False,
    )
```

time: 101 us -> 87.2 us (0.86); the launches traced: 100 us -> 85.6 us
  starting transfers between devices: 36.3 us -> 24.1 us
  Pallas kernels: 19.3 us -> 16.3 us
    ppermute x10 -> x8, starting transfers between devices: 28.6 us -> 17 us  [the longest x3 13 us: exchange(): lax.ppermute(far, 'pair', [(0, 0)] + inner + [(last, last)])]
    ppermute x10 -> x8, waiting for transfers between devices: 34.8 us -> 36.6 us  [the longest x3 34.8 us: exchange(): lax.ppermute(far, 'pair', [(0, 0)] + inner + [(last, last)])]
    pallas_call x2 -> x3, Pallas kernels: 9.87 us -> 8.24 us  [the longest x1 3.89 us: first_round(): pl.pallas_call(first_round_kernel, out_shape=[VMEM((CHUNKS[0], HALF), f32...]
    ppermute x6, waiting for transfers between devices: 9.19 us -> 7.63 us  [shifted(): lax.ppermute(value, 'row', [(at, (at + 2 * chips) % count) for at in rang...]
    pallas_call x1, Pallas kernels: 7.65 us -> 6.26 us  [second_round(): pl.pallas_call(functools.partial(second_round_kernel, len(parts)), out_sh...]
  transfers between devices with their start and end apart: 16 -> 14, of which waited for: 14 -> 11; matrix products, arithmetic and copies ran while one was open for 0% -> 0% of each run, Pallas kernels for 1% -> 3%
where the time goes in v3:
time: 87.2 us; the launch traced here: 85.6 us
  waiting for transfers between devices  44.2 us (51%)
  starting transfers between devices  24.1 us (28%)
  Pallas kernels  16.3 us (19%)
  between operations  0.89 us (1%)
    ppermute x3, waiting for transfers between devices, exchange(): lax.ppermute(far, 'pair', [(0, 0)] + inner + [(last, last)])  34.8 us
    ppermute x3, starting transfers between devices, exchange(): lax.ppermute(far, 'pair', [(0, 0)] + inner + [(last, last)])  13 us
    ppermute x6, waiting for transfers between devices, shifted(): lax.ppermute(value, 'row', [(at, (at + 2 * chips) % count) for at in rang...  7.63 us
    ppermute x6, starting transfers between devices, shifted(): lax.ppermute(value, 'row', [(at, (at + 2 * chips) % count) for at in rang...  7.08 us
    pallas_call x1, Pallas kernels, second_round(): pl.pallas_call(functools.partial(second_round_kernel, len(parts)), out_sh...  6.26 us
    pallas_call x1, Pallas kernels, first_round(): pl.pallas_call(first_round_kernel, out_shape=[VMEM((CHUNKS[0], HALF), f32...  3.89 us
    ppermute x2, starting transfers between devices, row_sum(): lax.ppermute(square, 'row', [(at, at ^ 1) for at in range(count)])  3.83 us
    pallas_call x1, Pallas kernels, first_gram(): pl.pallas_call(first_gram_kernel, out_shape=(SQUARE, VMEM(panel.shape, f3...  3.35 us
  transfers between devices with their start and end apart: 14, of which 11 were waited for; matrix products, arithmetic and copies ran while one was open for 0% of the time, Pallas kernels for 3%

profile of v3, /device:TPU:121, one launch (start us, length us, event | category | flops | bytes accessed | tf_op | source)
XLA Modules:
  0.0 85.6 jit_solution(1695726232275642204)
XLA Ops:
  0.6 0.0 copy-start
  0.6 3.4 %shard_map.41 = (f32[128,128]{1,0:T(8,128)S(1)}, f32[4096,256]{1,0:T(8,128)S(1)}) custom-call(f32[4096,256]{1,0:T(8,128)} %panel_hbm.1), custom_call_target="tpu_custom_call" | custom-call | flops 1610612736 | bytes 8388608 | tf_op jit(solution)/shard_map/pallas_call | solution.py:174
  4.0 0.8 collective-permute-start
  4.8 0.9 %collective-permute-done = f32[128,128]{1,0:T(8,128)S(1)} collective-permute-done((f32[128,128]{1,0:T(8,128)S(1)}, f32[128,128]{1,0:T(8,128)S(1)}, u32[]{:S(2)}, u32[]{:S(2)}) %collective-permute-start) | collective-permute-done | bytes 65568 | tf_op jit(solution)/shard_map/ppermute | solution.py:399
  5.7 2.8 %collective-permute-start.3 = (f32[128,128]{1,0:T(8,128)S(1)}, f32[128,128]{1,0:T(8,128)S(1)}, u32[]{:S(2)}, u32[]{:S(2)}) collective-permute-start(f32[128,128]{1,0:T(8,128)S(1)} %add.6.refs_2_), channel_id=1, source_target_pairs={{0,4},{1,5},{2,6},{3,7},{4,0},{5,1},{6,2},{7,3},{8,12},{9,13},{10,... | collective-permute-start | bytes 196616 | tf_op jit(solution)/shard_map/ppermute | solution.py:397
  8.5 0.9 %collective-permute-start.2 = (f32[128,128]{1,0:T(8,128)S(1)}, f32[128,128]{1,0:T(8,128)S(1)}, u32[]{:S(2)}, u32[]{:S(2)}) collective-permute-start(f32[128,128]{1,0:T(8,128)S(1)} %add.6.refs_2_), channel_id=1, source_target_pairs={{0,6},{1,7},{2,0},{3,1},{4,2},{5,3},{6,4},{7,5},{8,14},{9,15},{10,... | collective-permute-start | bytes 196616 | tf_op jit(solution)/shard_map/ppermute | solution.py:397
  9.4 0.6 collective-permute-start.1
  10.0 0.4 collective-permute-done.3.refs_3_
  10.4 1.6 %collective-permute-done.2.refs_1_ = f32[128,128]{1,0:T(8,128)S(1)} collective-permute-done((f32[128,128]{1,0:T(8,128)S(1)}, f32[128,128]{1,0:T(8,128)S(1)}, u32[]{:S(2)}, u32[]{:S(2)}) %collective-permute-start.2) | collective-permute-done | bytes 65568 | tf_op jit(solution)/shard_map/ppermute | solution.py:397
  12.0 1.7 %collective-permute-done.1.refs_0_ = f32[128,128]{1,0:T(8,128)S(1)} collective-permute-done((f32[128,128]{1,0:T(8,128)S(1)}, f32[128,128]{1,0:T(8,128)S(1)}, u32[]{:S(2)}, u32[]{:S(2)}) %collective-permute-start.1) | collective-permute-done | bytes 65568 | tf_op jit(solution)/shard_map/ppermute | solution.py:397
  13.7 3.9 %shard_map.42 = (f32[2048,128]{1,0:T(8,128)S(1)}, f32[2048,128]{1,0:T(8,128)S(1)}, bf16[256,256]{1,0:T(8,128)(2,1)S(1)}, bf16[256,256]{1,0:T(8,128)(2,1)S(1)}) custom-call(f32[128,128]{1,0:T(8,128)S(1)} %collective-permute-done.1.refs_0_, f32[128,128]{1,0:T(8,128)S(1)} %collective-permute-done.2.refs_1_, f32[128,128]{1,0:T(8,128)S(1)} %add.6.refs_2_, ...), custom_call_target="tpu_custom_call" | custom-call | tf_op jit(solution)/shard_map/pallas_call | solution.py:324
  17.6 4.4 %collective-permute-start.4 = (f32[2048,128]{1,0:T(8,128)S(1)}, f32[2048,128]{1,0:T(8,128)S(1)}, u32[]{:S(2)}, u32[]{:S(2)}) collective-permute-start(f32[2048,128]{1,0:T(8,128)S(1)} %get-tuple-element.16), channel_id=1, source_target_pairs={{0,0},{8,16},{16,8},{24,32},{32,24},{40,48},{48,40},{56,64},{64,56... | collective-permute-start | bytes 3145736 | tf_op jit(solution)/shard_map/ppermute | solution.py:412
  22.0 0.1 collective-permute-start.5
  22.1 1.0 %shard_map.44 = (f32[1024,128]{1,0:T(8,128)S(1)}, f32[1024,128]{1,0:T(8,128)S(1)}, f32[1024,128]{1,0:T(8,128)S(1)}, f32[1024,128]{1,0:T(8,128)S(1)}) custom-call(bf16[256,256]{1,0:T(8,128)(2,1)S(1)} %get-tuple-element.18.high_ref, bf16[256,256]{1,0:T(8,128)(2,1)S(1)} %get-tuple-element.19.low_ref, f32[4096,256]{1,0:T(8,128)S(1)} %get-tuple-element.15.refs_5_.panel_ref), custom_call_target="tpu_custom_call" | custom-call | flops 805306368 | bytes 4194304 | tf_op jit(solution)/shard_map/pallas_call | solution.py:332
  23.1 4.5 %collective-permute-start.6 = (f32[1024,128]{1,0:T(8,128)S(1)}, f32[1024,128]{1,0:T(8,128)S(1)}, u32[]{:S(2)}, u32[]{:S(2)}) collective-permute-start(f32[1024,128]{1,0:T(8,128)S(1)} %get-tuple-element.20), channel_id=1, source_target_pairs={{0,0},{8,16},{16,8},{24,32},{32,24},{40,48},{48,40},{56,64},{64,56... | collective-permute-start | bytes 1572872 | tf_op jit(solution)/shard_map/ppermute | solution.py:412
  27.6 0.1 collective-permute-start.7
  27.7 4.1 %collective-permute-start.8 = (f32[1024,128]{1,0:T(8,128)S(1)}, f32[1024,128]{1,0:T(8,128)S(1)}, u32[]{:S(2)}, u32[]{:S(2)}) collective-permute-start(f32[1024,128]{1,0:T(8,128)S(1)} %get-tuple-element.22), channel_id=1, source_target_pairs={{0,0},{8,16},{16,8},{24,32},{32,24},{40,48},{48,40},{56,64},{64,56... | collective-permute-start | bytes 1572872 | tf_op jit(solution)/shard_map/ppermute | solution.py:412
  31.8 13.6 %collective-permute-done.4.refs_0_.refs_5_ = f32[2048,128]{1,0:T(8,128)S(1)} collective-permute-done((f32[2048,128]{1,0:T(8,128)S(1)}, f32[2048,128]{1,0:T(8,128)S(1)}, u32[]{:S(2)}, u32[]{:S(2)}) %collective-permute-start.4) | collective-permute-done | bytes 1048608 | tf_op jit(solution)/shard_map/ppermute | solution.py:412
  45.4 0.7 shard_map.43.refs_0_
  46.1 10.5 %collective-permute-done.6.refs_1_.refs_7_ = f32[1024,128]{1,0:T(8,128)S(1)} collective-permute-done((f32[1024,128]{1,0:T(8,128)S(1)}, f32[1024,128]{1,0:T(8,128)S(1)}, u32[]{:S(2)}, u32[]{:S(2)}) %collective-permute-start.6) | collective-permute-done | bytes 524320 | tf_op jit(solution)/shard_map/ppermute | solution.py:412
  56.6 0.5 shard_map.45.refs_0_
  57.1 10.8 %collective-permute-done.8.refs_1_.refs_9_ = f32[1024,128]{1,0:T(8,128)S(1)} collective-permute-done((f32[1024,128]{1,0:T(8,128)S(1)}, f32[1024,128]{1,0:T(8,128)S(1)}, u32[]{:S(2)}, u32[]{:S(2)}) %collective-permute-start.8) | collective-permute-done | bytes 524320 | tf_op jit(solution)/shard_map/ppermute | solution.py:412
  67.9 0.6 shard_map.46
  68.5 3.1 %collective-permute-start.10 = (f32[128,128]{1,0:T(8,128)S(1)}, f32[128,128]{1,0:T(8,128)S(1)}, u32[]{:S(2)}, u32[]{:S(2)}) collective-permute-start(f32[128,128]{1,0:T(8,128)S(1)} %shard_map.46), channel_id=1, source_target_pairs={{0,1},{1,0},{2,3},{3,2},{4,5},{5,4},{6,7},{7,6},{8,9},{9,8},{10,11... | collective-permute-start | bytes 196616 | tf_op jit(solution)/shard_map/ppermute | solution.py:399
  71.6 0.9 %collective-permute-done.10 = f32[128,128]{1,0:T(8,128)S(1)} collective-permute-done((f32[128,128]{1,0:T(8,128)S(1)}, f32[128,128]{1,0:T(8,128)S(1)}, u32[]{:S(2)}, u32[]{:S(2)}) %collective-permute-start.10) | collective-permute-done | bytes 65568 | tf_op jit(solution)/shard_map/ppermute | solution.py:399
  72.5 1.3 %collective-permute-start.13 = (f32[128,128]{1,0:T(8,128)S(1)}, f32[128,128]{1,0:T(8,128)S(1)}, u32[]{:S(2)}, u32[]{:S(2)}) collective-permute-start(f32[128,128]{1,0:T(8,128)S(1)} %add.7.refs_2_), channel_id=1, source_target_pairs={{0,4},{1,5},{2,6},{3,7},{4,0},{5,1},{6,2},{7,3},{8,12},{9,13},{10,... | collective-permute-start | bytes 196616 | tf_op jit(solution)/shard_map/ppermute | solution.py:397
  73.8 1.0 %collective-permute-start.12 = (f32[128,128]{1,0:T(8,128)S(1)}, f32[128,128]{1,0:T(8,128)S(1)}, u32[]{:S(2)}, u32[]{:S(2)}) collective-permute-start(f32[128,128]{1,0:T(8,128)S(1)} %add.7.refs_2_), channel_id=1, source_target_pairs={{0,6},{1,7},{2,0},{3,1},{4,2},{5,3},{6,4},{7,5},{8,14},{9,15},{10,... | collective-permute-start | bytes 196616 | tf_op jit(solution)/shard_map/ppermute | solution.py:397
  74.8 0.4 collective-permute-start.11
  75.3 1.9 %collective-permute-done.13.refs_3_ = f32[128,128]{1,0:T(8,128)S(1)} collective-permute-done((f32[128,128]{1,0:T(8,128)S(1)}, f32[128,128]{1,0:T(8,128)S(1)}, u32[]{:S(2)}, u32[]{:S(2)}) %collective-permute-start.13) | collective-permute-done | bytes 65568 | tf_op jit(solution)/shard_map/ppermute | solution.py:397
  77.2 0.7 collective-permute-done.12.refs_1_
  77.9 1.3 %collective-permute-done.11.refs_0_ = f32[128,128]{1,0:T(8,128)S(1)} collective-permute-done((f32[128,128]{1,0:T(8,128)S(1)}, f32[128,128]{1,0:T(8,128)S(1)}, u32[]{:S(2)}, u32[]{:S(2)}) %collective-permute-start.11) | collective-permute-done | bytes 65568 | tf_op jit(solution)/shard_map/ppermute | solution.py:397
  79.2 6.3 %shard_map.47 = (f32[4096,256]{1,0:T(8,128)}, f32[1,256]{1,0:T(1,128)}) custom-call(f32[128,128]{1,0:T(8,128)S(1)} %collective-permute-done.11.refs_0_, f32[128,128]{1,0:T(8,128)S(1)} %collective-permute-done.12.refs_1_, f32[128,128]{1,0:T(8,128)S(1)} %add.7.refs_2_, f32[128,128]{1,0:T(8,128)S(1)} %collective-permute-done.13.refs_3_, ...), custom_call_target="tpu_custom_call" | custom-call | tf_op jit(solution)/shard_map/pallas_call | solution.py:383
  (7 shorter events, 0.0 us)
Async XLA Ops:
  0.6 13.1 %copy-start = (bf16[256,256]{1,0:T(8,128)(2,1)S(1)}, bf16[256,256]{1,0:T(8,128)(2,1)}, u32[]{:S(2)}) copy-start(bf16[256,256]{1,0:T(8,128)(2,1)} %constant.2.clone.refs_4_) | copy-start | bytes 393220
  4.0 1.7 %collective-permute-start = (f32[128,128]{1,0:T(8,128)S(1)}, f32[128,128]{1,0:T(8,128)S(1)}, u32[]{:S(2)}, u32[]{:S(2)}) collective-permute-start(f32[128,128]{1,0:T(8,128)S(1)} %get-tuple-element.14), channel_id=1, source_target_pairs={{0,1},{1,0},{2,3},{3,2},{4,5},{5,4},{6,7},{7,6},{8,9},{9,8},{10,11... | collective-permute-start | bytes 196616 | tf_op jit(solution)/shard_map/ppermute | solution.py:399
  5.7 4.7 %collective-permute-start.3 = (f32[128,128]{1,0:T(8,128)S(1)}, f32[128,128]{1,0:T(8,128)S(1)}, u32[]{:S(2)}, u32[]{:S(2)}) collective-permute-start(f32[128,128]{1,0:T(8,128)S(1)} %add.6.refs_2_), channel_id=1, source_target_pairs={{0,4},{1,5},{2,6},{3,7},{4,0},{5,1},{6,2},{7,3},{8,12},{9,13},{10,... | collective-permute-start | bytes 196616 | tf_op jit(solution)/shard_map/ppermute | solution.py:397
  8.5 3.5 %collective-permute-start.2 = (f32[128,128]{1,0:T(8,128)S(1)}, f32[128,128]{1,0:T(8,128)S(1)}, u32[]{:S(2)}, u32[]{:S(2)}) collective-permute-start(f32[128,128]{1,0:T(8,128)S(1)} %add.6.refs_2_), channel_id=1, source_target_pairs={{0,6},{1,7},{2,0},{3,1},{4,2},{5,3},{6,4},{7,5},{8,14},{9,15},{10,... | collective-permute-start | bytes 196616 | tf_op jit(solution)/shard_map/ppermute | solution.py:397
  9.4 4.3 %collective-permute-start.1 = (f32[128,128]{1,0:T(8,128)S(1)}, f32[128,128]{1,0:T(8,128)S(1)}, u32[]{:S(2)}, u32[]{:S(2)}) collective-permute-start(f32[128,128]{1,0:T(8,128)S(1)} %add.6.refs_2_), channel_id=1, source_target_pairs={{0,2},{1,3},{2,4},{3,5},{4,6},{5,7},{6,0},{7,1},{8,10},{9,11},{10,... | collective-permute-start | bytes 196616 | tf_op jit(solution)/shard_map/ppermute | solution.py:397
  17.6 27.8 %collective-permute-start.4 = (f32[2048,128]{1,0:T(8,128)S(1)}, f32[2048,128]{1,0:T(8,128)S(1)}, u32[]{:S(2)}, u32[]{:S(2)}) collective-permute-start(f32[2048,128]{1,0:T(8,128)S(1)} %get-tuple-element.16), channel_id=1, source_target_pairs={{0,0},{8,16},{16,8},{24,32},{32,24},{40,48},{48,40},{56,64},{64,56... | collective-permute-start | bytes 3145736 | tf_op jit(solution)/shard_map/ppermute | solution.py:412
  22.0 23.4 %collective-permute-start.5 = (f32[2048,128]{1,0:T(8,128)S(1)}, f32[2048,128]{1,0:T(8,128)S(1)}, u32[]{:S(2)}, u32[]{:S(2)}) collective-permute-start(f32[2048,128]{1,0:T(8,128)S(1)} %get-tuple-element.17), channel_id=1, source_target_pairs={{0,8},{8,0},{16,24},{24,16},{32,40},{40,32},{48,56},{56,48},{64,72... | collective-permute-start | bytes 3145736 | tf_op jit(solution)/shard_map/ppermute | solution.py:413
  23.1 33.5 %collective-permute-start.6 = (f32[1024,128]{1,0:T(8,128)S(1)}, f32[1024,128]{1,0:T(8,128)S(1)}, u32[]{:S(2)}, u32[]{:S(2)}) collective-permute-start(f32[1024,128]{1,0:T(8,128)S(1)} %get-tuple-element.20), channel_id=1, source_target_pairs={{0,0},{8,16},{16,8},{24,32},{32,24},{40,48},{48,40},{56,64},{64,56... | collective-permute-start | bytes 1572872 | tf_op jit(solution)/shard_map/ppermute | solution.py:412
  27.6 29.0 %collective-permute-start.7 = (f32[1024,128]{1,0:T(8,128)S(1)}, f32[1024,128]{1,0:T(8,128)S(1)}, u32[]{:S(2)}, u32[]{:S(2)}) collective-permute-start(f32[1024,128]{1,0:T(8,128)S(1)} %get-tuple-element.21), channel_id=1, source_target_pairs={{0,8},{8,0},{16,24},{24,16},{32,40},{40,32},{48,56},{56,48},{64,72... | collective-permute-start | bytes 1572872 | tf_op jit(solution)/shard_map/ppermute | solution.py:413
  27.7 40.1 %collective-permute-start.8 = (f32[1024,128]{1,0:T(8,128)S(1)}, f32[1024,128]{1,0:T(8,128)S(1)}, u32[]{:S(2)}, u32[]{:S(2)}) collective-permute-start(f32[1024,128]{1,0:T(8,128)S(1)} %get-tuple-element.22), channel_id=1, source_target_pairs={{0,0},{8,16},{16,8},{24,32},{32,24},{40,48},{48,40},{56,64},{64,56... | collective-permute-start | bytes 1572872 | tf_op jit(solution)/shard_map/ppermute | solution.py:412
  45.4 22.5 %collective-permute-start.9 = (f32[1024,128]{1,0:T(8,128)S(1)}, f32[1024,128]{1,0:T(8,128)S(1)}, u32[]{:S(2)}, u32[]{:S(2)}) collective-permute-start(f32[1024,128]{1,0:T(8,128)S(1)} %get-tuple-element.23), channel_id=1, source_target_pairs={{0,8},{8,0},{16,24},{24,16},{32,40},{40,32},{48,56},{56,48},{64,72... | collective-permute-start | bytes 1572872 | tf_op jit(solution)/shard_map/ppermute | solution.py:413
  68.5 4.0 %collective-permute-start.10 = (f32[128,128]{1,0:T(8,128)S(1)}, f32[128,128]{1,0:T(8,128)S(1)}, u32[]{:S(2)}, u32[]{:S(2)}) collective-permute-start(f32[128,128]{1,0:T(8,128)S(1)} %shard_map.46), channel_id=1, source_target_pairs={{0,1},{1,0},{2,3},{3,2},{4,5},{5,4},{6,7},{7,6},{8,9},{9,8},{10,11... | collective-permute-start | bytes 196616 | tf_op jit(solution)/shard_map/ppermute | solution.py:399
  72.5 4.7 %collective-permute-start.13 = (f32[128,128]{1,0:T(8,128)S(1)}, f32[128,128]{1,0:T(8,128)S(1)}, u32[]{:S(2)}, u32[]{:S(2)}) collective-permute-start(f32[128,128]{1,0:T(8,128)S(1)} %add.7.refs_2_), channel_id=1, source_target_pairs={{0,4},{1,5},{2,6},{3,7},{4,0},{5,1},{6,2},{7,3},{8,12},{9,13},{10,... | collective-permute-start | bytes 196616 | tf_op jit(solution)/shard_map/ppermute | solution.py:397
  73.8 4.1 %collective-permute-start.12 = (f32[128,128]{1,0:T(8,128)S(1)}, f32[128,128]{1,0:T(8,128)S(1)}, u32[]{:S(2)}, u32[]{:S(2)}) collective-permute-start(f32[128,128]{1,0:T(8,128)S(1)} %add.7.refs_2_), channel_id=1, source_target_pairs={{0,6},{1,7},{2,0},{3,1},{4,2},{5,3},{6,4},{7,5},{8,14},{9,15},{10,... | collective-permute-start | bytes 196616 | tf_op jit(solution)/shard_map/ppermute | solution.py:397
  74.8 4.3 %collective-permute-start.11 = (f32[128,128]{1,0:T(8,128)S(1)}, f32[128,128]{1,0:T(8,128)S(1)}, u32[]{:S(2)}, u32[]{:S(2)}) collective-permute-start(f32[128,128]{1,0:T(8,128)S(1)} %add.7.refs_2_), channel_id=1, source_target_pairs={{0,2},{1,3},{2,4},{3,5},{4,6},{5,7},{6,0},{7,1},{8,10},{9,11},{10,... | collective-permute-start | bytes 196616 | tf_op jit(solution)/shard_map/ppermute | solution.py:397

commit v4 on v3

--- a/solution.py
+++ b/solution.py
@@ -10,10 +10,11 @@
 
 STEPS = 16
 HALF = 128
-REACH = 2 * STEPS - 1
+SPAN = 2 * STEPS
+REACH = SPAN - 1
 CHUNK = 512
 GRAM_CHUNK = 1024
-CHUNKS = (2048, 1024, 1024)
+CHUNKS = (1024, 1024, 1024, 1024)
 f32 = jnp.float32
 bf16 = jnp.bfloat16
 
@@ -54,19 +55,31 @@
     return across, down
 
 
-def pack(gram, swapped, square_ref):
-    first = jnp.where(swapped, gram[HALF:, HALF:], gram[:HALF, :HALF])
-    second = jnp.where(swapped, gram[:HALF, :HALF], gram[HALF:, HALF:])
-    cross = jnp.where(swapped, gram[HALF:, :HALF], gram[:HALF, HALF:])
+def pack(total_ref, swapped, square_ref):
+    def block(row, column):
+        rows, columns = pl.ds(row * HALF, HALF), pl.ds(column * HALF, HALF)
+        mixed = total_ref[rows, pl.ds((2 + column) * HALF, HALF)]
+        turned = total_ref[columns, pl.ds((2 + row) * HALF, HALF)].T
+        return total_ref[rows, columns] + (mixed + turned)
+
+    first, second, cross = block(0, 0), block(1, 1), block(0, 1)
+    if swapped is not None:
+        first, second = jnp.where(swapped, second, first), jnp.where(swapped, first, second)
+        cross = jnp.where(swapped, cross.T, cross)
     across, down = grid_of(HALF)
     ahead = (across - down) & (HALF - 1)
-    square_ref[...] = jnp.where(
+    square = jnp.where(
         jnp.logical_or(ahead < REACH, ahead > HALF - REACH),
         cross,
-        jnp.where(
-            ahead < 2 * REACH, pltpu.roll(first, REACH, 1), pltpu.roll(second, 2 * REACH, 1)
-        ),
-    )
+        jnp.where(ahead < 2 * SPAN, pltpu.roll(first, SPAN, 1), pltpu.roll(second, 2 * SPAN, 1)),
+    )
+    square_ref[:SPAN] = square[:SPAN]
+    square_ref[SPAN : 2 * SPAN] = jnp.where(
+        (ahead[:SPAN] & 1) == 0,
+        square[SPAN : 2 * SPAN],
+        pltpu.roll(square[2 * SPAN : 3 * SPAN], 1, 1),
+    )
+    square_ref[2 * SPAN :] = square[3 * SPAN :]
 
 
 def fold(value):
@@ -79,9 +92,20 @@
     return jnp.where(near, jnp.concatenate([value, value], axis=0), 0.0)
 
 
-def unpack(square, lead_ref, trail_ref):
+def unpack(packed, lead_ref, trail_ref):
     across, down = grid_of(HALF)
     ahead = across - down
+    even = (ahead[:SPAN] & 1) == 0
+    shared = packed[SPAN : 2 * SPAN]
+    square = jnp.concatenate(
+        [
+            packed[:SPAN],
+            jnp.where(even, shared, 0.0),
+            pltpu.roll(jnp.where(even, 0.0, shared), HALF - 1, 1),
+            packed[2 * SPAN :],
+        ],
+        axis=0,
+    )
 
     def symmetric(moved):
         upper = pltpu.roll(square, HALF - moved, 1)
@@ -89,21 +113,15 @@
         return fold(jnp.where(ahead >= 0, upper, upper.T))
 
     cross = jnp.where(jnp.abs(ahead) < REACH, square, 0.0)
-    lead_ref[: HALF // 2] = symmetric(REACH)
+    lead_ref[: HALF // 2] = symmetric(SPAN)
     lead_ref[HALF // 2 :] = fold(cross.T)
     trail_ref[: HALF // 2] = fold(cross)
-    trail_ref[HALF // 2 :] = symmetric(2 * REACH)
+    trail_ref[HALF // 2 :] = symmetric(2 * SPAN)
 
 
 def add_gram(total_ref, panel):
     high, low = split(panel)
     total_ref[...] += dot_rows(high, jnp.concatenate([high, low], axis=1))
-
-
-def finish_gram(total_ref, swapped, square_ref):
-    mixed = total_ref[:, 2 * HALF :]
-    gram = total_ref[:, : 2 * HALF] + (mixed + mixed.T)
-    pack(gram, swapped, square_ref)
 
 
 def first_gram_kernel(panel_hbm, square_ref, panel_ref, total_ref, sems):
@@ -117,7 +135,7 @@
     for rows, copy in copies:
         copy.wait()
         add_gram(total_ref, panel_ref[rows])
-    finish_gram(total_ref, False, square_ref)
+    pack(total_ref, None, square_ref)
 
 
 def is_odd():
@@ -140,11 +158,11 @@
         rows = pl.ds(number * GRAM_CHUNK, GRAM_CHUNK)
         add_gram(total_ref, jnp.concatenate([far_ref[rows], near_ref[rows]], axis=1))
     if is_last:
-        finish_gram(total_ref, is_odd(), square_ref)
+        pack(total_ref, is_odd(), square_ref)
 
 
 VMEM = pltpu.VMEM
-SQUARE = VMEM((HALF, HALF), f32)
+SQUARE = VMEM((3 * SPAN, HALF), f32)
 TOTAL = VMEM((2 * HALF, 4 * HALF), f32)
 IN_VMEM = pl.BlockSpec(memory_space=pltpu.VMEM)
 IN_HBM = pl.BlockSpec(memory_space=pltpu.HBM)
@@ -214,7 +232,7 @@
     up_size = jnp.abs(up)
     scale = jnp.maximum(along_size, up_size)
     flat = scale == 0.0
-    inverse = 1.0 / jnp.where(flat, 1.0, scale)
+    inverse = pl.reciprocal(jnp.where(flat, 1.0, scale), approx=True)
     along_part = jnp.where(flat, 1.0, along_size * inverse)
     up_part = up_size * inverse
     length = lax.rsqrt(along_part * along_part + up_part * up_part)

time: 87.2 us -> 86.3 us (0.990)
  waiting for transfers between devices: 44.2 us -> 39.1 us
  starting transfers between devices: 24.1 us -> 27.8 us
    ppermute x3 -> x4, waiting for transfers between devices: 34.8 us -> 29.7 us  [exchange(): lax.ppermute(far, 'pair', [(0, 0)] + inner + [(last, last)])]
    ppermute x3 -> x4, starting transfers between devices: 13 us -> 17.4 us  [exchange(): lax.ppermute(far, 'pair', [(0, 0)] + inner + [(last, last)])]
    pallas_call x3 -> x4, Pallas kernels: 1.81 us -> 2.08 us  [second_gram(): pl.pallas_call(functools.partial(second_gram_kernel, before is None, is_l...]
  transfers between devices with their start and end apart: 14 -> 16, of which waited for: 11 -> 11; matrix products, arithmetic and copies ran while one was open for 0% -> 0% of each run, Pallas kernels for 3% -> 3%
where the time goes in v4:
time: 86.3 us; the launch traced here: 84.7 us
  waiting for transfers between devices  39.1 us (45%)
  starting transfers between devices  27.8 us (32%)
  Pallas kernels  16.8 us (19%)
  between operations  0.9 us (1%)
    ppermute x4, waiting for transfers between devices, exchange(): lax.ppermute(far, 'pair', [(0, 0)] + inner + [(last, last)])  29.7 us
    ppermute x4, starting transfers between devices, exchange(): lax.ppermute(far, 'pair', [(0, 0)] + inner + [(last, last)])  17.4 us
    ppermute x6, waiting for transfers between devices, shifted(): lax.ppermute(value, 'row', [(at, (at + 2 * chips) % count) for at in rang...  7.69 us
    ppermute x6, starting transfers between devices, shifted(): lax.ppermute(value, 'row', [(at, (at + 2 * chips) % count) for at in rang...  6.31 us
    pallas_call x1, Pallas kernels, second_round(): pl.pallas_call(functools.partial(second_round_kernel, len(parts)), out_sh...  6.3 us
    ppermute x2, starting transfers between devices, row_sum(): lax.ppermute(square, 'row', [(at, at ^ 1) for at in range(count)])  3.9 us
    pallas_call x1, Pallas kernels, first_round(): pl.pallas_call(first_round_kernel, out_shape=[VMEM((CHUNKS[0], HALF), f32...  3.54 us
    pallas_call x1, Pallas kernels, first_gram(): pl.pallas_call(first_gram_kernel, out_shape=(SQUARE, VMEM(panel.shape, f3...  3.45 us
  transfers between devices with their start and end apart: 16, of which 11 were waited for; matrix products, arithmetic and copies ran while one was open for 0% of the time, Pallas kernels for 3%

profile of v4, /device:TPU:121, one launch (start us, length us, event | category | flops | bytes accessed | tf_op | source)
XLA Modules:
  0.0 84.7 jit_solution(14149705412215182341)
XLA Ops:
  0.6 3.4 %shard_map.41 = (f32[96,128]{1,0:T(8,128)S(1)}, f32[4096,256]{1,0:T(8,128)S(1)}) custom-call(f32[4096,256]{1,0:T(8,128)} %panel_hbm.1), custom_call_target="tpu_custom_call" | custom-call | flops 1610612736 | bytes 8388608 | tf_op jit(solution)/shard_map/pallas_call | solution.py:192
  4.1 0.8 collective-permute-start
  4.9 0.9 %collective-permute-done = f32[96,128]{1,0:T(8,128)S(1)} collective-permute-done((f32[96,128]{1,0:T(8,128)S(1)}, f32[96,128]{1,0:T(8,128)S(1)}, u32[]{:S(2)}, u32[]{:S(2)}) %collective-permute-start) | collective-permute-done | bytes 49184 | tf_op jit(solution)/shard_map/ppermute | solution.py:417
  5.7 2.7 %collective-permute-start.3 = (f32[96,128]{1,0:T(8,128)S(1)}, f32[96,128]{1,0:T(8,128)S(1)}, u32[]{:S(2)}, u32[]{:S(2)}) collective-permute-start(f32[96,128]{1,0:T(8,128)S(1)} %add.6.refs_2_), channel_id=1, source_target_pairs={{0,4},{1,5},{2,6},{3,7},{4,0},{5,1},{6,2},{7,3},{8,12},{9,13},{10,... | collective-permute-start | bytes 147464 | tf_op jit(solution)/shard_map/ppermute | solution.py:415
  8.5 0.9 %collective-permute-start.2 = (f32[96,128]{1,0:T(8,128)S(1)}, f32[96,128]{1,0:T(8,128)S(1)}, u32[]{:S(2)}, u32[]{:S(2)}) collective-permute-start(f32[96,128]{1,0:T(8,128)S(1)} %add.6.refs_2_), channel_id=1, source_target_pairs={{0,6},{1,7},{2,0},{3,1},{4,2},{5,3},{6,4},{7,5},{8,14},{9,15},{10,... | collective-permute-start | bytes 147464 | tf_op jit(solution)/shard_map/ppermute | solution.py:415
  9.4 0.6 collective-permute-start.1
  10.0 0.2 collective-permute-done.3.refs_3_
  10.2 1.5 %collective-permute-done.2.refs_1_ = f32[96,128]{1,0:T(8,128)S(1)} collective-permute-done((f32[96,128]{1,0:T(8,128)S(1)}, f32[96,128]{1,0:T(8,128)S(1)}, u32[]{:S(2)}, u32[]{:S(2)}) %collective-permute-start.2) | collective-permute-done | bytes 49184 | tf_op jit(solution)/shard_map/ppermute | solution.py:415
  11.7 1.8 %collective-permute-done.1.refs_0_ = f32[96,128]{1,0:T(8,128)S(1)} collective-permute-done((f32[96,128]{1,0:T(8,128)S(1)}, f32[96,128]{1,0:T(8,128)S(1)}, u32[]{:S(2)}, u32[]{:S(2)}) %collective-permute-start.1) | collective-permute-done | bytes 49184 | tf_op jit(solution)/shard_map/ppermute | solution.py:415
  13.5 3.5 %shard_map.42 = (f32[1024,128]{1,0:T(8,128)S(1)}, f32[1024,128]{1,0:T(8,128)S(1)}, bf16[256,256]{1,0:T(8,128)(2,1)S(1)}, bf16[256,256]{1,0:T(8,128)(2,1)S(1)}) custom-call(f32[96,128]{1,0:T(8,128)S(1)} %collective-permute-done.1.refs_0_, f32[96,128]{1,0:T(8,128)S(1)} %collective-permute-done.2.refs_1_, f32[96,128]{1,0:T(8,128)S(1)} %add.6.refs_2_, ...), custom_call_target="tpu_custom_call" | custom-call | tf_op jit(solution)/shard_map/pallas_call | solution.py:342
  17.0 4.4 %collective-permute-start.4 = (f32[1024,128]{1,0:T(8,128)S(1)}, f32[1024,128]{1,0:T(8,128)S(1)}, u32[]{:S(2)}, u32[]{:S(2)}) collective-permute-start(f32[1024,128]{1,0:T(8,128)S(1)} %get-tuple-element.18), channel_id=1, source_target_pairs={{0,0},{8,16},{16,8},{24,32},{32,24},{40,48},{48,40},{56,64},{64,56... | collective-permute-start | bytes 1572872 | tf_op jit(solution)/shard_map/ppermute | solution.py:430
  21.5 0.1 collective-permute-start.5
  21.6 1.4 %shard_map.44 = (f32[1024,128]{1,0:T(8,128)S(1)}, f32[1024,128]{1,0:T(8,128)S(1)}, f32[1024,128]{1,0:T(8,128)S(1)}, f32[1024,128]{1,0:T(8,128)S(1)}, f32[1024,128]{1,0:T(8,128)S(1)}, /*index=5*/f32[1024,128]{1,0:T(8,128)S(1)}) custom-call(bf16[256,256]{1,0:T(8,128)(2,1)S(1)} %get-tuple-element.20.high_ref, bf16[256,256]{1,0:T(8,128)(2,1)S(1)} %get-tuple-element.21.low_ref, ...), custom_call_target="tpu_custom_call" | custom-call | flops 1207959552 | bytes 6291456 | tf_op jit(solution)/shard_map/pallas_call | solution.py:350
  23.0 4.5 %collective-permute-start.6 = (f32[1024,128]{1,0:T(8,128)S(1)}, f32[1024,128]{1,0:T(8,128)S(1)}, u32[]{:S(2)}, u32[]{:S(2)}) collective-permute-start(f32[1024,128]{1,0:T(8,128)S(1)} %get-tuple-element.22), channel_id=1, source_target_pairs={{0,0},{8,16},{16,8},{24,32},{32,24},{40,48},{48,40},{56,64},{64,56... | collective-permute-start | bytes 1572872 | tf_op jit(solution)/shard_map/ppermute | solution.py:430
  27.5 0.1 collective-permute-start.7
  27.6 4.1 %collective-permute-start.8 = (f32[1024,128]{1,0:T(8,128)S(1)}, f32[1024,128]{1,0:T(8,128)S(1)}, u32[]{:S(2)}, u32[]{:S(2)}) collective-permute-start(f32[1024,128]{1,0:T(8,128)S(1)} %get-tuple-element.24), channel_id=1, source_target_pairs={{0,0},{8,16},{16,8},{24,32},{32,24},{40,48},{48,40},{56,64},{64,56... | collective-permute-start | bytes 1572872 | tf_op jit(solution)/shard_map/ppermute | solution.py:430
  31.7 1.8 %collective-permute-done.4.refs_0_.refs_5_ = f32[1024,128]{1,0:T(8,128)S(1)} collective-permute-done((f32[1024,128]{1,0:T(8,128)S(1)}, f32[1024,128]{1,0:T(8,128)S(1)}, u32[]{:S(2)}, u32[]{:S(2)}) %collective-permute-start.4) | collective-permute-done | bytes 524320 | tf_op jit(solution)/shard_map/ppermute | solution.py:430
  33.5 4.4 %collective-permute-start.10 = (f32[1024,128]{1,0:T(8,128)S(1)}, f32[1024,128]{1,0:T(8,128)S(1)}, u32[]{:S(2)}, u32[]{:S(2)}) collective-permute-start(f32[1024,128]{1,0:T(8,128)S(1)} %get-tuple-element.26), channel_id=1, source_target_pairs={{0,0},{8,16},{16,8},{24,32},{32,24},{40,48},{48,40},{56,64},{64,56... | collective-permute-start | bytes 1572872 | tf_op jit(solution)/shard_map/ppermute | solution.py:430
  38.0 6.8 %collective-permute-done.6.refs_1_.refs_7_ = f32[1024,128]{1,0:T(8,128)S(1)} collective-permute-done((f32[1024,128]{1,0:T(8,128)S(1)}, f32[1024,128]{1,0:T(8,128)S(1)}, u32[]{:S(2)}, u32[]{:S(2)}) %collective-permute-start.6) | collective-permute-done | bytes 524320 | tf_op jit(solution)/shard_map/ppermute | solution.py:430
  44.8 0.5 shard_map.43.refs_0_
  45.3 0.5 shard_map.45.refs_0_
  45.7 10.3 %collective-permute-done.8.refs_1_.refs_9_ = f32[1024,128]{1,0:T(8,128)S(1)} collective-permute-done((f32[1024,128]{1,0:T(8,128)S(1)}, f32[1024,128]{1,0:T(8,128)S(1)}, u32[]{:S(2)}, u32[]{:S(2)}) %collective-permute-start.8) | collective-permute-done | bytes 524320 | tf_op jit(solution)/shard_map/ppermute | solution.py:430
  56.0 0.5 shard_map.46.refs_0_
  56.5 10.8 %collective-permute-done.10.refs_1_.refs_11_ = f32[1024,128]{1,0:T(8,128)S(1)} collective-permute-done((f32[1024,128]{1,0:T(8,128)S(1)}, f32[1024,128]{1,0:T(8,128)S(1)}, u32[]{:S(2)}, u32[]{:S(2)}) %collective-permute-start.10) | collective-permute-done | bytes 524320 | tf_op jit(solution)/shard_map/ppermute | solution.py:430
  67.3 0.7 shard_map.47
  67.9 3.1 %collective-permute-start.12 = (f32[96,128]{1,0:T(8,128)S(1)}, f32[96,128]{1,0:T(8,128)S(1)}, u32[]{:S(2)}, u32[]{:S(2)}) collective-permute-start(f32[96,128]{1,0:T(8,128)S(1)} %shard_map.47), channel_id=1, source_target_pairs={{0,1},{1,0},{2,3},{3,2},{4,5},{5,4},{6,7},{7,6},{8,9},{9,8},{10,11... | collective-permute-start | bytes 147464 | tf_op jit(solution)/shard_map/ppermute | solution.py:417
  71.1 0.9 %collective-permute-done.12 = f32[96,128]{1,0:T(8,128)S(1)} collective-permute-done((f32[96,128]{1,0:T(8,128)S(1)}, f32[96,128]{1,0:T(8,128)S(1)}, u32[]{:S(2)}, u32[]{:S(2)}) %collective-permute-start.12) | collective-permute-done | bytes 49184 | tf_op jit(solution)/shard_map/ppermute | solution.py:417
  72.0 0.6 collective-permute-start.15
  72.6 1.5 %collective-permute-start.14 = (f32[96,128]{1,0:T(8,128)S(1)}, f32[96,128]{1,0:T(8,128)S(1)}, u32[]{:S(2)}, u32[]{:S(2)}) collective-permute-start(f32[96,128]{1,0:T(8,128)S(1)} %add.7.refs_2_), channel_id=1, source_target_pairs={{0,6},{1,7},{2,0},{3,1},{4,2},{5,3},{6,4},{7,5},{8,14},{9,15},{10,... | collective-permute-start | bytes 147464 | tf_op jit(solution)/shard_map/ppermute | solution.py:415
  74.1 2.4 %collective-permute-done.15.refs_3_ = f32[96,128]{1,0:T(8,128)S(1)} collective-permute-done((f32[96,128]{1,0:T(8,128)S(1)}, f32[96,128]{1,0:T(8,128)S(1)}, u32[]{:S(2)}, u32[]{:S(2)}) %collective-permute-start.15) | collective-permute-done | bytes 49184 | tf_op jit(solution)/shard_map/ppermute | solution.py:415
  76.4 1.8 %collective-permute-done.13.refs_0_ = f32[96,128]{1,0:T(8,128)S(1)} collective-permute-done((f32[96,128]{1,0:T(8,128)S(1)}, f32[96,128]{1,0:T(8,128)S(1)}, u32[]{:S(2)}, u32[]{:S(2)}) %collective-permute-start.13) | collective-permute-done | bytes 49184 | tf_op jit(solution)/shard_map/ppermute | solution.py:415
  78.2 6.3 %shard_map.48 = (f32[4096,256]{1,0:T(8,128)}, f32[1,256]{1,0:T(1,128)}) custom-call(f32[96,128]{1,0:T(8,128)S(1)} %collective-permute-done.13.refs_0_, f32[96,128]{1,0:T(8,128)S(1)} %collective-permute-done.14.refs_1_, f32[96,128]{1,0:T(8,128)S(1)} %add.7.refs_2_, f32[96,128]{1,0:T(8,128)S(1)} %collective-permute-done.15.refs_3_, ...), custom_call_target="tpu_custom_call" | custom-call | tf_op jit(solution)/shard_map/pallas_call | solution.py:401
  (12 shorter events, 0.0 us)
Async XLA Ops:
  0.6 12.9 %copy-start = (bf16[256,256]{1,0:T(8,128)(2,1)S(1)}, bf16[256,256]{1,0:T(8,128)(2,1)}, u32[]{:S(2)}) copy-start(bf16[256,256]{1,0:T(8,128)(2,1)} %constant.2.clone.refs_4_) | copy-start | bytes 393220
  4.1 1.6 %collective-permute-start = (f32[96,128]{1,0:T(8,128)S(1)}, f32[96,128]{1,0:T(8,128)S(1)}, u32[]{:S(2)}, u32[]{:S(2)}) collective-permute-start(f32[96,128]{1,0:T(8,128)S(1)} %get-tuple-element.16), channel_id=1, source_target_pairs={{0,1},{1,0},{2,3},{3,2},{4,5},{5,4},{6,7},{7,6},{8,9},{9,8},{10,11... | collective-permute-start | bytes 147464 | tf_op jit(solution)/shard_map/ppermute | solution.py:417
  5.7 4.4 %collective-permute-start.3 = (f32[96,128]{1,0:T(8,128)S(1)}, f32[96,128]{1,0:T(8,128)S(1)}, u32[]{:S(2)}, u32[]{:S(2)}) collective-permute-start(f32[96,128]{1,0:T(8,128)S(1)} %add.6.refs_2_), channel_id=1, source_target_pairs={{0,4},{1,5},{2,6},{3,7},{4,0},{5,1},{6,2},{7,3},{8,12},{9,13},{10,... | collective-permute-start | bytes 147464 | tf_op jit(solution)/shard_map/ppermute | solution.py:415
  8.5 3.2 %collective-permute-start.2 = (f32[96,128]{1,0:T(8,128)S(1)}, f32[96,128]{1,0:T(8,128)S(1)}, u32[]{:S(2)}, u32[]{:S(2)}) collective-permute-start(f32[96,128]{1,0:T(8,128)S(1)} %add.6.refs_2_), channel_id=1, source_target_pairs={{0,6},{1,7},{2,0},{3,1},{4,2},{5,3},{6,4},{7,5},{8,14},{9,15},{10,... | collective-permute-start | bytes 147464 | tf_op jit(solution)/shard_map/ppermute | solution.py:415
  9.4 4.2 %collective-permute-start.1 = (f32[96,128]{1,0:T(8,128)S(1)}, f32[96,128]{1,0:T(8,128)S(1)}, u32[]{:S(2)}, u32[]{:S(2)}) collective-permute-start(f32[96,128]{1,0:T(8,128)S(1)} %add.6.refs_2_), channel_id=1, source_target_pairs={{0,2},{1,3},{2,4},{3,5},{4,6},{5,7},{6,0},{7,1},{8,10},{9,11},{10,... | collective-permute-start | bytes 147464 | tf_op jit(solution)/shard_map/ppermute | solution.py:415
  17.0 16.5 %collective-permute-start.4 = (f32[1024,128]{1,0:T(8,128)S(1)}, f32[1024,128]{1,0:T(8,128)S(1)}, u32[]{:S(2)}, u32[]{:S(2)}) collective-permute-start(f32[1024,128]{1,0:T(8,128)S(1)} %get-tuple-element.18), channel_id=1, source_target_pairs={{0,0},{8,16},{16,8},{24,32},{32,24},{40,48},{48,40},{56,64},{64,56... | collective-permute-start | bytes 1572872 | tf_op jit(solution)/shard_map/ppermute | solution.py:430
  21.5 12.1 %collective-permute-start.5 = (f32[1024,128]{1,0:T(8,128)S(1)}, f32[1024,128]{1,0:T(8,128)S(1)}, u32[]{:S(2)}, u32[]{:S(2)}) collective-permute-start(f32[1024,128]{1,0:T(8,128)S(1)} %get-tuple-element.19), channel_id=1, source_target_pairs={{0,8},{8,0},{16,24},{24,16},{32,40},{40,32},{48,56},{56,48},{64,72... | collective-permute-start | bytes 1572872 | tf_op jit(solution)/shard_map/ppermute | solution.py:431
  23.0 21.8 %collective-permute-start.6 = (f32[1024,128]{1,0:T(8,128)S(1)}, f32[1024,128]{1,0:T(8,128)S(1)}, u32[]{:S(2)}, u32[]{:S(2)}) collective-permute-start(f32[1024,128]{1,0:T(8,128)S(1)} %get-tuple-element.22), channel_id=1, source_target_pairs={{0,0},{8,16},{16,8},{24,32},{32,24},{40,48},{48,40},{56,64},{64,56... | collective-permute-start | bytes 1572872 | tf_op jit(solution)/shard_map/ppermute | solution.py:430
  27.5 17.8 %collective-permute-start.7 = (f32[1024,128]{1,0:T(8,128)S(1)}, f32[1024,128]{1,0:T(8,128)S(1)}, u32[]{:S(2)}, u32[]{:S(2)}) collective-permute-start(f32[1024,128]{1,0:T(8,128)S(1)} %get-tuple-element.23), channel_id=1, source_target_pairs={{0,8},{8,0},{16,24},{24,16},{32,40},{40,32},{48,56},{56,48},{64,72... | collective-permute-start | bytes 1572872 | tf_op jit(solution)/shard_map/ppermute | solution.py:431
  27.6 28.4 %collective-permute-start.8 = (f32[1024,128]{1,0:T(8,128)S(1)}, f32[1024,128]{1,0:T(8,128)S(1)}, u32[]{:S(2)}, u32[]{:S(2)}) collective-permute-start(f32[1024,128]{1,0:T(8,128)S(1)} %get-tuple-element.24), channel_id=1, source_target_pairs={{0,0},{8,16},{16,8},{24,32},{32,24},{40,48},{48,40},{56,64},{64,56... | collective-permute-start | bytes 1572872 | tf_op jit(solution)/shard_map/ppermute | solution.py:430
  33.5 22.5 %collective-permute-start.9 = (f32[1024,128]{1,0:T(8,128)S(1)}, f32[1024,128]{1,0:T(8,128)S(1)}, u32[]{:S(2)}, u32[]{:S(2)}) collective-permute-start(f32[1024,128]{1,0:T(8,128)S(1)} %get-tuple-element.25), channel_id=1, source_target_pairs={{0,8},{8,0},{16,24},{24,16},{32,40},{40,32},{48,56},{56,48},{64,72... | collective-permute-start | bytes 1572872 | tf_op jit(solution)/shard_map/ppermute | solution.py:431
  33.5 33.7 %collective-permute-start.10 = (f32[1024,128]{1,0:T(8,128)S(1)}, f32[1024,128]{1,0:T(8,128)S(1)}, u32[]{:S(2)}, u32[]{:S(2)}) collective-permute-start(f32[1024,128]{1,0:T(8,128)S(1)} %get-tuple-element.26), channel_id=1, source_target_pairs={{0,0},{8,16},{16,8},{24,32},{32,24},{40,48},{48,40},{56,64},{64,56... | collective-permute-start | bytes 1572872 | tf_op jit(solution)/shard_map/ppermute | solution.py:430
  44.8 22.5 %collective-permute-start.11 = (f32[1024,128]{1,0:T(8,128)S(1)}, f32[1024,128]{1,0:T(8,128)S(1)}, u32[]{:S(2)}, u32[]{:S(2)}) collective-permute-start(f32[1024,128]{1,0:T(8,128)S(1)} %get-tuple-element.27), channel_id=1, source_target_pairs={{0,8},{8,0},{16,24},{24,16},{32,40},{40,32},{48,56},{56,48},{64,72... | collective-permute-start | bytes 1572872 | tf_op jit(solution)/shard_map/ppermute | solution.py:431
  67.9 4.0 %collective-permute-start.12 = (f32[96,128]{1,0:T(8,128)S(1)}, f32[96,128]{1,0:T(8,128)S(1)}, u32[]{:S(2)}, u32[]{:S(2)}) collective-permute-start(f32[96,128]{1,0:T(8,128)S(1)} %shard_map.47), channel_id=1, source_target_pairs={{0,1},{1,0},{2,3},{3,2},{4,5},{5,4},{6,7},{7,6},{8,9},{9,8},{10,11... | collective-permute-start | bytes 147464 | tf_op jit(solution)/shard_map/ppermute | solution.py:417
  72.0 4.4 %collective-permute-start.15 = (f32[96,128]{1,0:T(8,128)S(1)}, f32[96,128]{1,0:T(8,128)S(1)}, u32[]{:S(2)}, u32[]{:S(2)}) collective-permute-start(f32[96,128]{1,0:T(8,128)S(1)} %add.7.refs_2_), channel_id=1, source_target_pairs={{0,4},{1,5},{2,6},{3,7},{4,0},{5,1},{6,2},{7,3},{8,12},{9,13},{10,... | collective-permute-start | bytes 147464 | tf_op jit(solution)/shard_map/ppermute | solution.py:415
  72.6 3.8 %collective-permute-start.14 = (f32[96,128]{1,0:T(8,128)S(1)}, f32[96,128]{1,0:T(8,128)S(1)}, u32[]{:S(2)}, u32[]{:S(2)}) collective-permute-start(f32[96,128]{1,0:T(8,128)S(1)} %add.7.refs_2_), channel_id=1, source_target_pairs={{0,6},{1,7},{2,0},{3,1},{4,2},{5,3},{6,4},{7,5},{8,14},{9,15},{10,... | collective-permute-start | bytes 147464 | tf_op jit(solution)/shard_map/ppermute | solution.py:415
  74.1 4.2 %collective-permute-start.13 = (f32[96,128]{1,0:T(8,128)S(1)}, f32[96,128]{1,0:T(8,128)S(1)}, u32[]{:S(2)}, u32[]{:S(2)}) collective-permute-start(f32[96,128]{1,0:T(8,128)S(1)} %add.7.refs_2_), channel_id=1, source_target_pairs={{0,2},{1,3},{2,4},{3,5},{4,6},{5,7},{6,0},{7,1},{8,10},{9,11},{10,... | collective-permute-start | bytes 147464 | tf_op jit(solution)/shard_map/ppermute | solution.py:415

commit v5 on v4

--- a/solution.py
+++ b/solution.py
@@ -14,7 +14,7 @@
 REACH = SPAN - 1
 CHUNK = 512
 GRAM_CHUNK = 1024
-CHUNKS = (1024, 1024, 1024, 1024)
+CHUNKS = (1024, 1024, 1536, 512)
 f32 = jnp.float32
 bf16 = jnp.bfloat16
 
@@ -154,8 +154,8 @@
         total_ref[...] = jnp.zeros_like(total_ref)
     else:
         total_ref[...] = before_ref[...]
-    for number in range(near_ref.shape[0] // GRAM_CHUNK):
-        rows = pl.ds(number * GRAM_CHUNK, GRAM_CHUNK)
+    for number in range(near_ref.shape[0] // CHUNK):
+        rows = pl.ds(number * CHUNK, CHUNK)
         add_gram(total_ref, jnp.concatenate([far_ref[rows], near_ref[rows]], axis=1))
     if is_last:
         pack(total_ref, is_odd(), square_ref)
@@ -415,12 +415,12 @@
         return lax.ppermute(value, "row", [(at, (at + 2 * chips) % count) for at in range(count)])
 
     square = square + lax.ppermute(square, "row", [(at, at ^ 1) for at in range(count)])
-    return shifted(square, 1), shifted(square, -1), square, shifted(square, 2)
+    return shifted(square, -1), shifted(square, 1), square, shifted(square, 2)
 
 
 def total_of(parts):
-    ahead, behind, own, across = [part[...] for part in parts]
-    return (ahead + behind) + (own + across)
+    behind, ahead, own, across = [part[...] for part in parts]
+    return (behind + ahead) + (own + across)
 
 
 def exchange(near, far):

time: 86.3 us -> 90.2 us (1.045)
  starting transfers between devices: 27.8 us -> 32.7 us
  waiting for transfers between devices: 39.1 us -> 38.1 us
    ppermute x4, waiting for transfers between devices: 0.01 us -> 29.5 us  [exchange(): lax.ppermute(near, 'pair', [(at, at ^ 1) for at in range(last + 1)])]
    ppermute x4, waiting for transfers between devices: 29.7 us -> 3.24 us  [exchange(): lax.ppermute(far, 'pair', [(0, 0)] + inner + [(last, last)])]
    ppermute x6, waiting for transfers between devices: 7.69 us -> 3.51 us  [shifted(): lax.ppermute(value, 'row', [(at, (at + 2 * chips) % count) for at in rang...]
    ppermute x6, starting transfers between devices: 6.31 us -> 9.58 us  [shifted(): lax.ppermute(value, 'row', [(at, (at + 2 * chips) % count) for at in rang...]
    ppermute x4, starting transfers between devices: 0.19 us -> 1.55 us  [exchange(): lax.ppermute(near, 'pair', [(at, at ^ 1) for at in range(last + 1)])]
where the time goes in v5:
time: 90.2 us; the launch traced here: 88.5 us
  waiting for transfers between devices  38.1 us (42%)
  starting transfers between devices  32.7 us (36%)
  Pallas kernels  16.8 us (19%)
  between operations  0.91 us (1%)
    ppermute x4, waiting for transfers between devices, exchange(): lax.ppermute(near, 'pair', [(at, at ^ 1) for at in range(last + 1)])  29.5 us
    ppermute x4, starting transfers between devices, exchange(): lax.ppermute(far, 'pair', [(0, 0)] + inner + [(last, last)])  17.4 us
    ppermute x6, starting transfers between devices, shifted(): lax.ppermute(value, 'row', [(at, (at + 2 * chips) % count) for at in rang...  9.58 us
    pallas_call x1, Pallas kernels, second_round(): pl.pallas_call(functools.partial(second_round_kernel, len(parts)), out_sh...  6.3 us
    ppermute x2, starting transfers between devices, row_sum(): lax.ppermute(square, 'row', [(at, at ^ 1) for at in range(count)])  4.18 us
    pallas_call x1, Pallas kernels, first_round(): pl.pallas_call(first_round_kernel, out_shape=[VMEM((CHUNKS[0], HALF), f32...  3.54 us
    ppermute x6, waiting for transfers between devices, shifted(): lax.ppermute(value, 'row', [(at, (at + 2 * chips) % count) for at in rang...  3.51 us
    pallas_call x1, Pallas kernels, first_gram(): pl.pallas_call(first_gram_kernel, out_shape=(SQUARE, VMEM(panel.shape, f3...  3.45 us
  transfers between devices with their start and end apart: 16, of which 11 were waited for; matrix products, arithmetic and copies ran while one was open for 0% of the time, Pallas kernels for 3%

profile of v5, /device:TPU:121, one launch (start us, length us, event | category | flops | bytes accessed | tf_op | source)
XLA Modules:
  0.0 88.5 jit_solution(13841701598988406731)
XLA Ops:
  0.6 3.4 %shard_map.41 = (f32[96,128]{1,0:T(8,128)S(1)}, f32[4096,256]{1,0:T(8,128)S(1)}) custom-call(f32[4096,256]{1,0:T(8,128)} %panel_hbm.1), custom_call_target="tpu_custom_call" | custom-call | flops 1610612736 | bytes 8388608 | tf_op jit(solution)/shard_map/pallas_call | solution.py:192
  4.1 0.8 collective-permute-start
  4.9 0.9 collective-permute-done
  5.7 2.7 %collective-permute-start.3 = (f32[96,128]{1,0:T(8,128)S(1)}, f32[96,128]{1,0:T(8,128)S(1)}, u32[]{:S(2)}, u32[]{:S(2)}) collective-permute-start(f32[96,128]{1,0:T(8,128)S(1)} %add.6.refs_2_), channel_id=1, source_target_pairs={{0,4},{1,5},{2,6},{3,7},{4,0},{5,1},{6,2},{7,3},{8,12},{9,13},{10,... | collective-permute-start | bytes 147464 | tf_op jit(solution)/shard_map/ppermute | solution.py:415
  8.5 0.3 collective-permute-start.2
  8.8 2.4 %collective-permute-start.1 = (f32[96,128]{1,0:T(8,128)S(1)}, f32[96,128]{1,0:T(8,128)S(1)}, u32[]{:S(2)}, u32[]{:S(2)}) collective-permute-start(f32[96,128]{1,0:T(8,128)S(1)} %add.6.refs_2_), channel_id=1, source_target_pairs={{0,6},{1,7},{2,0},{3,1},{4,2},{5,3},{6,4},{7,5},{8,14},{9,15},{10,... | collective-permute-start | bytes 147464 | tf_op jit(solution)/shard_map/ppermute | solution.py:415
  11.2 1.5 %collective-permute-done.2.refs_1_ = f32[96,128]{1,0:T(8,128)S(1)} collective-permute-done((f32[96,128]{1,0:T(8,128)S(1)}, f32[96,128]{1,0:T(8,128)S(1)}, u32[]{:S(2)}, u32[]{:S(2)}) %collective-permute-start.2) | collective-permute-done | bytes 49184 | tf_op jit(solution)/shard_map/ppermute | solution.py:415
  12.6 3.5 %shard_map.42 = (f32[1024,128]{1,0:T(8,128)S(1)}, f32[1024,128]{1,0:T(8,128)S(1)}, bf16[256,256]{1,0:T(8,128)(2,1)S(1)}, bf16[256,256]{1,0:T(8,128)(2,1)S(1)}) custom-call(f32[96,128]{1,0:T(8,128)S(1)} %collective-permute-done.1.refs_0_, f32[96,128]{1,0:T(8,128)S(1)} %collective-permute-done.2.refs_1_, f32[96,128]{1,0:T(8,128)S(1)} %add.6.refs_2_, ...), custom_call_target="tpu_custom_call" | custom-call | tf_op jit(solution)/shard_map/pallas_call | solution.py:342
  16.2 4.4 %collective-permute-start.4 = (f32[1024,128]{1,0:T(8,128)S(1)}, f32[1024,128]{1,0:T(8,128)S(1)}, u32[]{:S(2)}, u32[]{:S(2)}) collective-permute-start(f32[1024,128]{1,0:T(8,128)S(1)} %get-tuple-element.18), channel_id=1, source_target_pairs={{0,0},{8,16},{16,8},{24,32},{32,24},{40,48},{48,40},{56,64},{64,56... | collective-permute-start | bytes 1572872 | tf_op jit(solution)/shard_map/ppermute | solution.py:430
  20.6 1.4 %shard_map.44 = (f32[1024,128]{1,0:T(8,128)S(1)}, f32[1024,128]{1,0:T(8,128)S(1)}, f32[1536,128]{1,0:T(8,128)S(1)}, f32[1536,128]{1,0:T(8,128)S(1)}, f32[512,128]{1,0:T(8,128)S(1)}, /*index=5*/f32[512,128]{1,0:T(8,128)S(1)}) custom-call(bf16[256,256]{1,0:T(8,128)(2,1)S(1)} %get-tuple-element.20.high_ref, bf16[256,256]{1,0:T(8,128)(2,1)S(1)} %get-tuple-element.21.low_ref, ...), custom_call_target="tpu_custom_call" | custom-call | flops 1207959552 | bytes 6291456 | tf_op jit(solution)/shard_map/pallas_call | solution.py:350
  22.0 4.2 %collective-permute-start.8 = (f32[1536,128]{1,0:T(8,128)S(1)}, f32[1536,128]{1,0:T(8,128)S(1)}, u32[]{:S(2)}, u32[]{:S(2)}) collective-permute-start(f32[1536,128]{1,0:T(8,128)S(1)} %get-tuple-element.24), channel_id=1, source_target_pairs={{0,0},{8,16},{16,8},{24,32},{32,24},{40,48},{48,40},{56,64},{64,56... | collective-permute-start | bytes 2359304 | tf_op jit(solution)/shard_map/ppermute | solution.py:430
  26.3 1.5 %collective-permute-start.5 = (f32[1024,128]{1,0:T(8,128)S(1)}, f32[1024,128]{1,0:T(8,128)S(1)}, u32[]{:S(2)}, u32[]{:S(2)}) collective-permute-start(f32[1024,128]{1,0:T(8,128)S(1)} %get-tuple-element.19), channel_id=1, source_target_pairs={{0,8},{8,0},{16,24},{24,16},{32,40},{40,32},{48,56},{56,48},{64,72... | collective-permute-start | bytes 1572872 | tf_op jit(solution)/shard_map/ppermute | solution.py:431
  27.8 4.4 %collective-permute-start.6 = (f32[1024,128]{1,0:T(8,128)S(1)}, f32[1024,128]{1,0:T(8,128)S(1)}, u32[]{:S(2)}, u32[]{:S(2)}) collective-permute-start(f32[1024,128]{1,0:T(8,128)S(1)} %get-tuple-element.22), channel_id=1, source_target_pairs={{0,0},{8,16},{16,8},{24,32},{32,24},{40,48},{48,40},{56,64},{64,56... | collective-permute-start | bytes 1572872 | tf_op jit(solution)/shard_map/ppermute | solution.py:430
  32.2 0.8 collective-permute-done.4.refs_0_.refs_5_
  33.0 21.2 %collective-permute-done.5.refs_1_.refs_6_ = f32[1024,128]{1,0:T(8,128)S(1)} collective-permute-done((f32[1024,128]{1,0:T(8,128)S(1)}, f32[1024,128]{1,0:T(8,128)S(1)}, u32[]{:S(2)}, u32[]{:S(2)}) %collective-permute-start.5) | collective-permute-done | bytes 524320 | tf_op jit(solution)/shard_map/ppermute | solution.py:431
  54.1 4.4 %collective-permute-start.10 = (f32[512,128]{1,0:T(8,128)S(1)}, f32[512,128]{1,0:T(8,128)S(1)}, u32[]{:S(2)}, u32[]{:S(2)}) collective-permute-start(f32[512,128]{1,0:T(8,128)S(1)} %get-tuple-element.26), channel_id=1, source_target_pairs={{0,0},{8,16},{16,8},{24,32},{32,24},{40,48},{48,40},{56,64},{64,56... | collective-permute-start | bytes 786440 | tf_op jit(solution)/shard_map/ppermute | solution.py:430
  58.6 2.5 %collective-permute-done.6.refs_1_.refs_7_ = f32[1024,128]{1,0:T(8,128)S(1)} collective-permute-done((f32[1024,128]{1,0:T(8,128)S(1)}, f32[1024,128]{1,0:T(8,128)S(1)}, u32[]{:S(2)}, u32[]{:S(2)}) %collective-permute-start.6) | collective-permute-done | bytes 524320 | tf_op jit(solution)/shard_map/ppermute | solution.py:430
  61.0 0.5 shard_map.43.refs_0_
  61.5 3.9 %collective-permute-done.7.refs_2_.refs_8_ = f32[1024,128]{1,0:T(8,128)S(1)} collective-permute-done((f32[1024,128]{1,0:T(8,128)S(1)}, f32[1024,128]{1,0:T(8,128)S(1)}, u32[]{:S(2)}, u32[]{:S(2)}) %collective-permute-start.7) | collective-permute-done | bytes 524320 | tf_op jit(solution)/shard_map/ppermute | solution.py:431
  65.4 0.5 shard_map.45.refs_0_
  65.9 0.6 shard_map.46.refs_0_
  66.5 4.5 %collective-permute-done.11.refs_2_.refs_12_ = f32[512,128]{1,0:T(8,128)S(1)} collective-permute-done((f32[512,128]{1,0:T(8,128)S(1)}, f32[512,128]{1,0:T(8,128)S(1)}, u32[]{:S(2)}, u32[]{:S(2)}) %collective-permute-start.11) | collective-permute-done | bytes 262176 | tf_op jit(solution)/shard_map/ppermute | solution.py:431
  71.0 0.5 shard_map.47
  71.5 3.4 %collective-permute-start.12 = (f32[96,128]{1,0:T(8,128)S(1)}, f32[96,128]{1,0:T(8,128)S(1)}, u32[]{:S(2)}, u32[]{:S(2)}) collective-permute-start(f32[96,128]{1,0:T(8,128)S(1)} %shard_map.47), channel_id=1, source_target_pairs={{0,1},{1,0},{2,3},{3,2},{4,5},{5,4},{6,7},{7,6},{8,9},{9,8},{10,11... | collective-permute-start | bytes 147464 | tf_op jit(solution)/shard_map/ppermute | solution.py:417
  75.0 0.9 collective-permute-done.12
  75.8 1.5 %collective-permute-start.15 = (f32[96,128]{1,0:T(8,128)S(1)}, f32[96,128]{1,0:T(8,128)S(1)}, u32[]{:S(2)}, u32[]{:S(2)}) collective-permute-start(f32[96,128]{1,0:T(8,128)S(1)} %add.7.refs_2_), channel_id=1, source_target_pairs={{0,4},{1,5},{2,6},{3,7},{4,0},{5,1},{6,2},{7,3},{8,12},{9,13},{10,... | collective-permute-start | bytes 147464 | tf_op jit(solution)/shard_map/ppermute | solution.py:415
  77.3 1.8 %collective-permute-start.14 = (f32[96,128]{1,0:T(8,128)S(1)}, f32[96,128]{1,0:T(8,128)S(1)}, u32[]{:S(2)}, u32[]{:S(2)}) collective-permute-start(f32[96,128]{1,0:T(8,128)S(1)} %add.7.refs_2_), channel_id=1, source_target_pairs={{0,2},{1,3},{2,4},{3,5},{4,6},{5,7},{6,0},{7,1},{8,10},{9,11},{10,... | collective-permute-start | bytes 147464 | tf_op jit(solution)/shard_map/ppermute | solution.py:415
  79.1 0.9 %collective-permute-start.13 = (f32[96,128]{1,0:T(8,128)S(1)}, f32[96,128]{1,0:T(8,128)S(1)}, u32[]{:S(2)}, u32[]{:S(2)}) collective-permute-start(f32[96,128]{1,0:T(8,128)S(1)} %add.7.refs_2_), channel_id=1, source_target_pairs={{0,6},{1,7},{2,0},{3,1},{4,2},{5,3},{6,4},{7,5},{8,14},{9,15},{10,... | collective-permute-start | bytes 147464 | tf_op jit(solution)/shard_map/ppermute | solution.py:415
  80.0 0.3 collective-permute-done.15.refs_3_
  80.3 1.4 %collective-permute-done.14.refs_1_ = f32[96,128]{1,0:T(8,128)S(1)} collective-permute-done((f32[96,128]{1,0:T(8,128)S(1)}, f32[96,128]{1,0:T(8,128)S(1)}, u32[]{:S(2)}, u32[]{:S(2)}) %collective-permute-start.14) | collective-permute-done | bytes 49184 | tf_op jit(solution)/shard_map/ppermute | solution.py:415
  81.7 0.3 collective-permute-done.13.refs_0_
  82.0 6.3 %shard_map.48 = (f32[4096,256]{1,0:T(8,128)}, f32[1,256]{1,0:T(1,128)}) custom-call(f32[96,128]{1,0:T(8,128)S(1)} %collective-permute-done.13.refs_0_, f32[96,128]{1,0:T(8,128)S(1)} %collective-permute-done.14.refs_1_, f32[96,128]{1,0:T(8,128)S(1)} %add.7.refs_2_, f32[96,128]{1,0:T(8,128)S(1)} %collective-permute-done.15.refs_3_, ...), custom_call_target="tpu_custom_call" | custom-call | tf_op jit(solution)/shard_map/pallas_call | solution.py:401
  (12 shorter events, 0.1 us)
Async XLA Ops:
  0.6 12.0 %copy-start = (bf16[256,256]{1,0:T(8,128)(2,1)S(1)}, bf16[256,256]{1,0:T(8,128)(2,1)}, u32[]{:S(2)}) copy-start(bf16[256,256]{1,0:T(8,128)(2,1)} %constant.2.clone.refs_4_) | copy-start | bytes 393220
  4.1 1.6 %collective-permute-start = (f32[96,128]{1,0:T(8,128)S(1)}, f32[96,128]{1,0:T(8,128)S(1)}, u32[]{:S(2)}, u32[]{:S(2)}) collective-permute-start(f32[96,128]{1,0:T(8,128)S(1)} %get-tuple-element.16), channel_id=1, source_target_pairs={{0,1},{1,0},{2,3},{3,2},{4,5},{5,4},{6,7},{7,6},{8,9},{9,8},{10,11... | collective-permute-start | bytes 147464 | tf_op jit(solution)/shard_map/ppermute | solution.py:417
  5.7 5.4 %collective-permute-start.3 = (f32[96,128]{1,0:T(8,128)S(1)}, f32[96,128]{1,0:T(8,128)S(1)}, u32[]{:S(2)}, u32[]{:S(2)}) collective-permute-start(f32[96,128]{1,0:T(8,128)S(1)} %add.6.refs_2_), channel_id=1, source_target_pairs={{0,4},{1,5},{2,6},{3,7},{4,0},{5,1},{6,2},{7,3},{8,12},{9,13},{10,... | collective-permute-start | bytes 147464 | tf_op jit(solution)/shard_map/ppermute | solution.py:415
  8.5 4.2 %collective-permute-start.2 = (f32[96,128]{1,0:T(8,128)S(1)}, f32[96,128]{1,0:T(8,128)S(1)}, u32[]{:S(2)}, u32[]{:S(2)}) collective-permute-start(f32[96,128]{1,0:T(8,128)S(1)} %add.6.refs_2_), channel_id=1, source_target_pairs={{0,2},{1,3},{2,4},{3,5},{4,6},{5,7},{6,0},{7,1},{8,10},{9,11},{10,... | collective-permute-start | bytes 147464 | tf_op jit(solution)/shard_map/ppermute | solution.py:415
  8.8 3.8 %collective-permute-start.1 = (f32[96,128]{1,0:T(8,128)S(1)}, f32[96,128]{1,0:T(8,128)S(1)}, u32[]{:S(2)}, u32[]{:S(2)}) collective-permute-start(f32[96,128]{1,0:T(8,128)S(1)} %add.6.refs_2_), channel_id=1, source_target_pairs={{0,6},{1,7},{2,0},{3,1},{4,2},{5,3},{6,4},{7,5},{8,14},{9,15},{10,... | collective-permute-start | bytes 147464 | tf_op jit(solution)/shard_map/ppermute | solution.py:415
  16.2 16.8 %collective-permute-start.4 = (f32[1024,128]{1,0:T(8,128)S(1)}, f32[1024,128]{1,0:T(8,128)S(1)}, u32[]{:S(2)}, u32[]{:S(2)}) collective-permute-start(f32[1024,128]{1,0:T(8,128)S(1)} %get-tuple-element.18), channel_id=1, source_target_pairs={{0,0},{8,16},{16,8},{24,32},{32,24},{40,48},{48,40},{56,64},{64,56... | collective-permute-start | bytes 1572872 | tf_op jit(solution)/shard_map/ppermute | solution.py:430
  22.0 43.8 %collective-permute-start.8 = (f32[1536,128]{1,0:T(8,128)S(1)}, f32[1536,128]{1,0:T(8,128)S(1)}, u32[]{:S(2)}, u32[]{:S(2)}) collective-permute-start(f32[1536,128]{1,0:T(8,128)S(1)} %get-tuple-element.24), channel_id=1, source_target_pairs={{0,0},{8,16},{16,8},{24,32},{32,24},{40,48},{48,40},{56,64},{64,56... | collective-permute-start | bytes 2359304 | tf_op jit(solution)/shard_map/ppermute | solution.py:430
  26.2 39.7 %collective-permute-start.9 = (f32[1536,128]{1,0:T(8,128)S(1)}, f32[1536,128]{1,0:T(8,128)S(1)}, u32[]{:S(2)}, u32[]{:S(2)}) collective-permute-start(f32[1536,128]{1,0:T(8,128)S(1)} %get-tuple-element.25), channel_id=1, source_target_pairs={{0,8},{8,0},{16,24},{24,16},{32,40},{40,32},{48,56},{56,48},{64,72... | collective-permute-start | bytes 2359304 | tf_op jit(solution)/shard_map/ppermute | solution.py:431
  26.3 27.8 %collective-permute-start.5 = (f32[1024,128]{1,0:T(8,128)S(1)}, f32[1024,128]{1,0:T(8,128)S(1)}, u32[]{:S(2)}, u32[]{:S(2)}) collective-permute-start(f32[1024,128]{1,0:T(8,128)S(1)} %get-tuple-element.19), channel_id=1, source_target_pairs={{0,8},{8,0},{16,24},{24,16},{32,40},{40,32},{48,56},{56,48},{64,72... | collective-permute-start | bytes 1572872 | tf_op jit(solution)/shard_map/ppermute | solution.py:431
  27.8 33.3 %collective-permute-start.6 = (f32[1024,128]{1,0:T(8,128)S(1)}, f32[1024,128]{1,0:T(8,128)S(1)}, u32[]{:S(2)}, u32[]{:S(2)}) collective-permute-start(f32[1024,128]{1,0:T(8,128)S(1)} %get-tuple-element.22), channel_id=1, source_target_pairs={{0,0},{8,16},{16,8},{24,32},{32,24},{40,48},{48,40},{56,64},{64,56... | collective-permute-start | bytes 1572872 | tf_op jit(solution)/shard_map/ppermute | solution.py:430
  33.0 32.4 %collective-permute-start.7 = (f32[1024,128]{1,0:T(8,128)S(1)}, f32[1024,128]{1,0:T(8,128)S(1)}, u32[]{:S(2)}, u32[]{:S(2)}) collective-permute-start(f32[1024,128]{1,0:T(8,128)S(1)} %get-tuple-element.23), channel_id=1, source_target_pairs={{0,8},{8,0},{16,24},{24,16},{32,40},{40,32},{48,56},{56,48},{64,72... | collective-permute-start | bytes 1572872 | tf_op jit(solution)/shard_map/ppermute | solution.py:431
  54.1 12.3 %collective-permute-start.10 = (f32[512,128]{1,0:T(8,128)S(1)}, f32[512,128]{1,0:T(8,128)S(1)}, u32[]{:S(2)}, u32[]{:S(2)}) collective-permute-start(f32[512,128]{1,0:T(8,128)S(1)} %get-tuple-element.26), channel_id=1, source_target_pairs={{0,0},{8,16},{16,8},{24,32},{32,24},{40,48},{48,40},{56,64},{64,56... | collective-permute-start | bytes 786440 | tf_op jit(solution)/shard_map/ppermute | solution.py:430
  61.0 10.0 %collective-permute-start.11 = (f32[512,128]{1,0:T(8,128)S(1)}, f32[512,128]{1,0:T(8,128)S(1)}, u32[]{:S(2)}, u32[]{:S(2)}) collective-permute-start(f32[512,128]{1,0:T(8,128)S(1)} %get-tuple-element.27), channel_id=1, source_target_pairs={{0,8},{8,0},{16,24},{24,16},{32,40},{40,32},{48,56},{56,48},{64,72... | collective-permute-start | bytes 786440 | tf_op jit(solution)/shard_map/ppermute | solution.py:431
  71.5 4.3 %collective-permute-start.12 = (f32[96,128]{1,0:T(8,128)S(1)}, f32[96,128]{1,0:T(8,128)S(1)}, u32[]{:S(2)}, u32[]{:S(2)}) collective-permute-start(f32[96,128]{1,0:T(8,128)S(1)} %shard_map.47), channel_id=1, source_target_pairs={{0,1},{1,0},{2,3},{3,2},{4,5},{5,4},{6,7},{7,6},{8,9},{9,8},{10,11... | collective-permute-start | bytes 147464 | tf_op jit(solution)/shard_map/ppermute | solution.py:417
  75.8 4.4 %collective-permute-start.15 = (f32[96,128]{1,0:T(8,128)S(1)}, f32[96,128]{1,0:T(8,128)S(1)}, u32[]{:S(2)}, u32[]{:S(2)}) collective-permute-start(f32[96,128]{1,0:T(8,128)S(1)} %add.7.refs_2_), channel_id=1, source_target_pairs={{0,4},{1,5},{2,6},{3,7},{4,0},{5,1},{6,2},{7,3},{8,12},{9,13},{10,... | collective-permute-start | bytes 147464 | tf_op jit(solution)/shard_map/ppermute | solution.py:415
  77.3 4.4 %collective-permute-start.14 = (f32[96,128]{1,0:T(8,128)S(1)}, f32[96,128]{1,0:T(8,128)S(1)}, u32[]{:S(2)}, u32[]{:S(2)}) collective-permute-start(f32[96,128]{1,0:T(8,128)S(1)} %add.7.refs_2_), channel_id=1, source_target_pairs={{0,2},{1,3},{2,4},{3,5},{4,6},{5,7},{6,0},{7,1},{8,10},{9,11},{10,... | collective-permute-start | bytes 147464 | tf_op jit(solution)/shard_map/ppermute | solution.py:415
  79.1 2.9 %collective-permute-start.13 = (f32[96,128]{1,0:T(8,128)S(1)}, f32[96,128]{1,0:T(8,128)S(1)}, u32[]{:S(2)}, u32[]{:S(2)}) collective-permute-start(f32[96,128]{1,0:T(8,128)S(1)} %add.7.refs_2_), channel_id=1, source_target_pairs={{0,6},{1,7},{2,0},{3,1},{4,2},{5,3},{6,4},{7,5},{8,14},{9,15},{10,... | collective-permute-start | bytes 147464 | tf_op jit(solution)/shard_map/ppermute | solution.py:415
